TPU v7x, 256 devices: a whole 4x4x8 slice. The times are simulated.
256 devices in a mesh: seq: 16 (over x_lo, z), expert: 16 (over x_hi, y, core).
Axes of the slice: x: 4 (x_hi: 2, x_lo: 2; x = x_hi * 2 + x_lo), y: 4, z: 8, core: 2. Of those that a mesh axis runs over, the one named last changes fastest.
Arguments:
- queries: bfloat16 [2048, 2, 8192], P('seq', None, 'expert'), may hold values from -8 to 8
- keys: bfloat16 [2048, 2, 512], P('seq'), may hold values from -8 to 8
- values: bfloat16 [2048, 2, 512], P('seq'), may hold values from -6 to 6
- prefix_keys: bfloat16 [64, 512], replicated, may hold values from -6 to 6
- prefix_values: bfloat16 [64, 512], replicated, may hold values from -6 to 6
- out_weight: bfloat16 [8192, 4096], P('expert', 'seq'), may hold values from -0.0625 to 0.0625
- residual_in: bfloat16 [2048, 2, 4096], P(('seq', 'expert')), may hold values from -8 to 8
- norm_gain: bfloat16 [4096], replicated, may hold values from 0.25 to 1.75
- expert_ids: int32 [2048, 2, 8], P(('seq', 'expert')), may hold values from 0 to 63, all different within a row; in each aligned block of 16 rows (0 to 15, 16 to 31, ..., all dimensions but the last counted through in order) at most 3 rows name the same one
- route_weights: float32 [2048, 2, 8], P(('seq', 'expert')), may hold values from 0.05 to 1
- w_gate: bfloat16 [16, 16, 4096, 384], P('seq', 'expert'), may hold values from -0.09375 to 0.09375
- w_up: bfloat16 [16, 16, 4096, 384], P('seq', 'expert'), may hold values from -0.09375 to 0.09375
- w_down: bfloat16 [16, 16, 384, 4096], P('seq', 'expert'), may hold values from -0.15625 to 0.15625
Outputs:
- mixed: bfloat16 [2048, 2, 4096], P(('seq', 'expert'))
Inputs may be any that keep to these rules, and one draw needn't show every extreme that they name: `expert_ids`: each token names 8 different experts; among the 16 tokens of one device (aligned blocks of 16 rows in position then sequence order) no expert is named more than 3 times.
All inputs are finite; a program needn't handle non-finite values.
Results may differ from a plain program's by a relative error of at most 0.019.
Values may be sent and summed in bfloat16 or wider, within the bound.
A program may use at most 128 MiB of HBM per device.

v0:
```python
import math

import jax
import jax.numpy as jnp
from jax import lax
from jax.sharding import PartitionSpec as P

D = 4096
HD = 128
KV = 4
EXP_DEV = 4
TOPK = 8


def shards(
    queries,
    keys,
    values,
    prefix_keys,
    prefix_values,
    out_weight,
    residual_in,
    norm_gain,
    expert_ids,
    route_weights,
    w_gate,
    w_up,
    w_down,
):
    seq_count = lax.axis_size("seq")
    expert_count = lax.axis_size("expert")
    seq_place = lax.axis_index("seq")
    expert_place = lax.axis_index("expert")
    block_len, seq_num, query_width = queries.shape
    heads_local = query_width // HD
    head_group = heads_local * expert_count // KV
    shared_head = expert_place * heads_local // head_group
    own_keys = lax.dynamic_slice_in_dim(keys, shared_head * HD, HD, 2)
    own_values = lax.dynamic_slice_in_dim(values, shared_head * HD, HD, 2)
    prefix_key = lax.dynamic_slice_in_dim(prefix_keys, shared_head * HD, HD, 1)
    prefix_value = lax.dynamic_slice_in_dim(prefix_values, shared_head * HD, HD, 1)
    score_scale = 1.0 / math.sqrt(HD)
    grouped_q = queries.reshape(block_len, seq_num, heads_local, HD)
    prefix_scores = (
        jnp.einsum("ibhd,pd->bhip", grouped_q, prefix_key, preferred_element_type=jnp.float32)
        * score_scale
    )
    prefix_top = jnp.max(prefix_scores, -1)
    prefix_weights = jnp.exp(prefix_scores - prefix_top[..., None]).astype(jnp.bfloat16)
    prefix_total = jnp.sum(prefix_weights, -1, dtype=jnp.float32)
    prefix_sum = jnp.einsum(
        "bhip,pd->bhid", prefix_weights, prefix_value, preferred_element_type=jnp.float32
    )
    query_places = seq_place * block_len + jnp.arange(block_len, dtype=jnp.int32)
    row_top = prefix_top
    row_total = prefix_total
    weighted = prefix_sum
    piece_keys = lax.all_gather(own_keys, "seq", axis=0, tiled=True)
    piece_values = lax.all_gather(own_values, "seq", axis=0, tiled=True)
    key_count = piece_keys.shape[0]
    scores = (
        jnp.einsum("ibhd,jbd->bhij", grouped_q, piece_keys, preferred_element_type=jnp.float32)
        * score_scale
    )
    key_places = jnp.arange(key_count, dtype=jnp.int32)
    allowed = key_places[None, :] <= query_places[:, None]
    scores = jnp.where(allowed, scores, -1e30)
    new_top = jnp.maximum(row_top, jnp.max(scores, -1))
    probabilities = jnp.exp(scores - new_top[..., None]).astype(jnp.bfloat16)
    shrink = jnp.exp(row_top - new_top)
    row_total = row_total * shrink + jnp.sum(probabilities, -1, dtype=jnp.float32)
    weighted = weighted * shrink[..., None] + jnp.einsum(
        "bhij,jbd->bhid", probabilities, piece_values, preferred_element_type=jnp.float32
    )
    row_top, row_total, weighted = (new_top, row_total, weighted)
    attended = (weighted / row_total[..., None]).astype(jnp.bfloat16)
    attended = jnp.transpose(attended, (2, 0, 1, 3)).reshape(block_len * seq_num, heads_local * HD)
    term_rows = jnp.dot(
        attended,
        lax.all_gather(out_weight, "seq", axis=1, tiled=True),
        preferred_element_type=jnp.float32,
    )
    summed = lax.psum_scatter(
        term_rows.astype(jnp.bfloat16), "expert", scatter_dimension=0, tiled=True
    ).astype(jnp.float32)
    hidden_state = residual_in.reshape(-1, D).astype(jnp.float32) + summed
    square = jnp.mean(hidden_state * hidden_state, -1, keepdims=True)
    normed = (hidden_state * lax.rsqrt(square + 1e-06) * norm_gain.astype(jnp.float32)).astype(
        jnp.bfloat16
    )
    token_count = hidden_state.shape[0]
    experts = EXP_DEV * expert_count
    capacity = max(2, 3 * token_count * TOPK // (2 * experts))
    slot_count = experts * capacity
    route_list = expert_ids.reshape(token_count * TOPK)
    expert_match = (route_list[:, None] == jnp.arange(experts, dtype=jnp.int32)[None, :]).astype(
        jnp.int32
    )
    rank_in = jnp.sum(jnp.cumsum(expert_match, 0) * expert_match, 1) - 1
    slot_index = (route_list % EXP_DEV * expert_count + route_list // EXP_DEV) * capacity + rank_in
    slot_match = (slot_index[:, None] == jnp.arange(slot_count, dtype=jnp.int32)[None, :]).reshape(
        token_count, TOPK, slot_count
    )
    dispatch_rows = jnp.sum(slot_match.astype(jnp.float32), 1).astype(jnp.bfloat16)
    combine_rows = jnp.sum(
        slot_match.astype(jnp.float32) * route_weights.reshape(token_count, TOPK, 1), 1
    )
    outgoing = jnp.einsum(
        "ts,td->sd", dispatch_rows, normed, preferred_element_type=jnp.float32
    ).astype(jnp.bfloat16)
    outgoing = outgoing.reshape(EXP_DEV, expert_count, capacity, D)
    arrived = lax.all_to_all(outgoing, "expert", split_axis=1, concat_axis=1, tiled=True)
    gate_weight = w_gate[0, 0]
    up_weight = w_up[0, 0]
    down_weight = w_down[0, 0]
    slices = seq_count // EXP_DEV
    spread = jnp.repeat(arrived, slices, axis=0)
    rows_in = lax.all_to_all(spread, "seq", split_axis=0, concat_axis=0, tiled=True)
    row_block = rows_in.reshape(-1, D)
    gate_proj = jnp.dot(row_block, gate_weight, preferred_element_type=jnp.float32)
    up_proj = jnp.dot(row_block, up_weight, preferred_element_type=jnp.float32)
    hidden = (jax.nn.silu(gate_proj) * up_proj).astype(jnp.bfloat16)
    partial_value = (
        jnp.dot(hidden, down_weight, preferred_element_type=jnp.float32)
        .astype(jnp.bfloat16)
        .reshape(seq_count, expert_count, capacity, D)
    )
    returned_parts = lax.all_to_all(partial_value, "seq", split_axis=0, concat_axis=0, tiled=True)
    expert_sum = jnp.sum(
        returned_parts.reshape(EXP_DEV, slices, expert_count, capacity, D), 1, dtype=jnp.float32
    )
    outputs = expert_sum.astype(jnp.bfloat16)
    returned = lax.all_to_all(outputs, "expert", split_axis=1, concat_axis=1, tiled=True)
    expert_mix = jnp.dot(
        combine_rows,
        returned.reshape(slot_count, D).astype(jnp.float32),
        precision=lax.Precision.HIGHEST,
    )
    return (hidden_state + expert_mix).astype(jnp.bfloat16).reshape(residual_in.shape)


def solution(mesh):
    in_specs = (
        P("seq", None, "expert"),
        P("seq", None, None),
        P("seq", None, None),
        P(),
        P(),
        P("expert", "seq"),
        P(("seq", "expert"), None, None),
        P(),
        P(("seq", "expert"), None, None),
        P(("seq", "expert"), None, None),
        P("seq", "expert", None, None),
        P("seq", "expert", None, None),
        P("seq", "expert", None, None),
    )
    out_specs = P(("seq", "expert"), None, None)
    return jax.shard_map(shards, mesh=mesh, in_specs=in_specs, out_specs=out_specs, check_vma=False)
```

profile of v0, /device:TPU:1, one launch (start us, length us, event | category | flops | bytes accessed | tf_op | source)
XLA Modules:
  0.0 761.8 jit_solution(16724658500941264518)
XLA Ops:
  14.6 57.3 %all-gather.4.cloned.1.call-done = bf16[2048,2,128]{2,0,1:T(8,128)(2,1)} async-done(((bf16[128,2,128]{2,0,1:T(8,128)(2,1)}), bf16[2048,2,128]{2,0,1:T(8,128)(2,1)}) %all-gather.4.cloned.1.call-update) | async-done | bytes 1048592 | tf_op jit(solution)/shard_map/all_gather | solution.py:58
  71.8 2.7 fusion
  79.6 60.7 %all-gather.6.cloned.1.call-done = bf16[2048,2,128]{2,0,1:T(8,128)(2,1)} async-done(((bf16[128,2,128]{2,0,1:T(8,128)(2,1)}), bf16[2048,2,128]{2,0,1:T(8,128)(2,1)}) %all-gather.6.cloned.1.call-update) | async-done | bytes 1048592 | tf_op jit(solution)/shard_map/all_gather | solution.py:59
  140.4 6.3 fusion.16
  146.8 82.9 %all-gather.8.cloned.1.call-done = bf16[512,4096]{1,0:T(8,128)(2,1)} async-done(((bf16[512,256]{1,0:T(8,128)(2,1)}), bf16[512,4096]{1,0:T(8,128)(2,1)}) %all-gather.8.cloned.1.call-update) | async-done | bytes 4194320 | tf_op jit(solution)/shard_map/all_gather | solution.py:80
  229.7 4.8 convolution_convert_fusion.1
  237.5 82.8 %reduce-scatter.2.cloned.1.call-done = bf16[16,4096]{1,0:T(8,128)(2,1)} async-done(((bf16[256,4096]{1,0:T(8,128)(2,1)}), bf16[16,4096]{1,0:T(8,128)(2,1)}) %reduce-scatter.2.cloned.1.call-update) | async-done | bytes 131088 | tf_op jit(solution)/shard_map/reduce_scatter | solution.py:83
  321.3 2.7 convolution_convert_fusion.2
  324.0 4.1 reshape.141
  328.1 3.2 copy.54
  331.3 29.4 %all_to_all.20 = bf16[4,16,3,4096]{3,0,2,1:T(4,128)(2,1)S(1)} all-to-all(bf16[4,16,3,4096]{3,0,2,1:T(4,128)(2,1)S(1)} %copy.54), channel_id=1, replica_groups=mesh['seq'=16,'expert'=16] {'expert'}, dimensions={1} | all-to-all | bytes 3145728 | tf_op jit(solution)/shard_map/all_to_all | solution.py:112
  362.4 143.3 %all_to_all.21 = bf16[16,16,3,4096]{3,1,2,0:T(8,128)(2,1)} all-to-all(bf16[16,16,3,4096]{3,1,2,0:T(8,128)(2,1)S(1)} %bitcast.89), channel_id=1, replica_groups=mesh['seq'=16,'expert'=16] {'seq'}, dimensions={0} | all-to-all | bytes 12582912 | tf_op jit(solution)/shard_map/all_to_all | solution.py:118
  505.7 11.5 %copy.56 = bf16[16,16,3,4096]{3,2,1,0:T(4,128)(2,1)} copy(bf16[16,16,3,4096]{3,1,2,0:T(8,128)(2,1)} %all_to_all.21) | data formatting | bytes 12582912 | tf_op jit(solution)/shard_map/all_to_all | solution.py:118
  517.2 13.7 %reshape.143 = bf16[768,4096]{1,0:T(8,128)(2,1)} reshape(bf16[16,16,3,4096]{3,2,1,0:T(4,128)(2,1)} %copy.56) | data formatting | bytes 12582912 | tf_op jit(solution)/shard_map/reshape | solution.py:119
  531.0 6.6 fusion.5
  537.6 3.5 fusion.10
  541.0 5.3 convolution_convert_fusion
  546.3 12.9 %reshape.144 = bf16[16,16,3,4096]{3,2,1,0:T(4,128)(2,1)} reshape(bf16[768,4096]{1,0:T(8,128)(2,1)} %convolution_convert_fusion) | data formatting | bytes 12582912 | tf_op jit(solution)/shard_map/reshape | solution.py:126
  559.2 8.5 %copy.57 = bf16[16,16,3,4096]{3,1,2,0:T(8,128)(2,1)S(1)} copy(bf16[16,16,3,4096]{3,2,1,0:T(4,128)(2,1)} %reshape.144) | data formatting | bytes 12582912 | tf_op jit(solution)/shard_map/reshape | solution.py:126
  567.7 142.4 %all_to_all.22 = bf16[16,16,3,4096]{3,1,2,0:T(8,128)(2,1)S(1)} all-to-all(bf16[16,16,3,4096]{3,1,2,0:T(8,128)(2,1)S(1)} %copy.57), channel_id=1, replica_groups=mesh['seq'=16,'expert'=16] {'seq'}, dimensions={0} | all-to-all | bytes 12582912 | tf_op jit(solution)/shard_map/all_to_all | solution.py:128
  712.5 31.3 %all_to_all.23 = bf16[4,16,3,4096]{3,0,2,1:T(4,128)(2,1)S(1)} all-to-all(bf16[4,16,3,4096]{3,0,2,1:T(4,128)(2,1)S(1)} %copy.58), channel_id=1, replica_groups=mesh['seq'=16,'expert'=16] {'expert'}, dimensions={1} | all-to-all | bytes 3145728 | tf_op jit(solution)/shard_map/all_to_all | solution.py:133
  743.8 2.7 copy.59
  746.5 4.3 reshape.146
  750.8 2.8 fusion.1
  (55 shorter events, 22.8 us)
Async XLA Ops:
  6.5 534.5 %copy-start = (bf16[1,1,384,4096]{3,2,1,0:T(8,128)(2,1)S(1)}, bf16[1,1,384,4096]{3,2,1,0:T(8,128)(2,1)}, u32[]{:S(2)}) copy-start(bf16[1,1,384,4096]{3,2,1,0:T(8,128)(2,1)} %param.25) | copy-start | bytes 9437188
  6.5 65.3 %all-gather.4.cloned.1.call-start = ((), (), s32[]{:S(2)}) async-start(), calls=%async_computation.5 | async-start | bytes 1114112 | tf_op jit(solution)/shard_map/all_gather | solution.py:58
  8.2 132.1 %all-gather.6.cloned.1.call-start = ((), (), s32[]{:S(2)}) async-start(), calls=%async_computation.6 | async-start | bytes 1114112 | tf_op jit(solution)/shard_map/all_gather | solution.py:59
  9.8 219.9 %all-gather.8.cloned.1.call-start = ((), (), s32[]{:S(2)}) async-start(), calls=%async_computation.7 | async-start | bytes 4456448 | tf_op jit(solution)/shard_map/all_gather | solution.py:80
  10.6 309.7 %reduce-scatter.2.cloned.1.call-start = ((), (), s32[]{:S(2)}) async-start(), calls=%async_computation.8 | async-start | bytes 2228224 | tf_op jit(solution)/shard_map/reduce_scatter | solution.py:83
  71.8 2.8 copy-start.4
  74.6 3.2 copy-start.1
  229.7 4.9 copy-start.6
  229.7 6.8 copy-start.5
  530.9 6.6 copy-start.2
  531.0 6.6 copy-start.7
  743.8 7.0 copy-start.3
Sparse Core Ops, SparseCore 0:
  9.2 62.6 all-gather.3
  73.6 66.6 all-gather.5
  142.1 87.5 all-gather.7
  234.7 85.5 reduce-scatter.1
where the time goes:
time: 763 us; the launch traced here: 762 us
  blocking collectives  346 us (45%)
  waiting for transfers between devices  284 us (37%)
  local copies, waits for them, and re-layouts  72.3 us (9%)
  matrix products  37.7 us (5%)
  between operations  13.3 us (2%)
    all_to_all x1, blocking collectives, shards(): lax.all_to_all(spread, 'seq', split_axis=0, concat_axis=0, tiled=True)  143 us
    all_to_all x1, blocking collectives, shards(): lax.all_to_all(partial_value, 'seq', split_axis=0, concat_axis=0, tiled=T...  142 us
    all_gather x1, waiting for transfers between devices, shards(): lax.all_gather(out_weight, 'seq', axis=1, tiled=True)  82.9 us
    reduce_scatter x1, waiting for transfers between devices, shards(): lax.psum_scatter(term_rows.astype(jnp.bfloat16), 'expert', scatter_dimens...  82.8 us
    all_gather x1, waiting for transfers between devices, shards(): piece_values = lax.all_gather(own_values, 'seq', axis=0, tiled=True)  60.7 us
    all_gather x1, waiting for transfers between devices, shards(): piece_keys = lax.all_gather(own_keys, 'seq', axis=0, tiled=True)  57.3 us
    all_to_all x1, blocking collectives, shards(): lax.all_to_all(outputs, 'expert', split_axis=1, concat_axis=1, tiled=True)  31.3 us
    all_to_all x1, blocking collectives, shards(): lax.all_to_all(outgoing, 'expert', split_axis=1, concat_axis=1, tiled=True)  29.4 us
  transfers between devices with their start and end apart: 4, of which 4 were waited for; matrix products, arithmetic and copies ran while one was open for 3% of the time, Pallas kernels for 0%

commit v1 on v0

--- a/solution.py
+++ b/solution.py
@@ -3,6 +3,8 @@
 import jax
 import jax.numpy as jnp
 from jax import lax
+from jax.experimental import pallas as pl
+from jax.experimental.pallas import tpu as pltpu
 from jax.sharding import PartitionSpec as P
 
 D = 4096
@@ -10,6 +12,478 @@
 KV = 4
 EXP_DEV = 4
 TOPK = 8
+
+
+MESH = pl.DeviceIdType.MESH
+BF = jnp.bfloat16
+F32 = jnp.float32
+NT = (((1,), (1,)), ((), ()))
+ORDER = (0, 1, 3, 2)
+SPOS = {0: 0, 1: 1, 3: 2, 2: 3}
+MOE_SEMS = 160
+
+
+def place():
+    s = lax.axis_index("seq")
+    e = lax.axis_index("expert")
+    return (e // 8) * 2 + s // 8, (e // 2) % 4, s % 8, e % 2
+
+
+def device(x, y, z, c):
+    return ((x % 2) * 8 + z, ((x // 2) * 4 + y) * 2 + c)
+
+
+class Links:
+    def __init__(self, send_sems, recv_sems):
+        self.send_sems = send_sems
+        self.recv_sems = recv_sems
+        self.used = 0
+        self.open = []
+
+    def send(self, src, dst, peer):
+        index = self.used
+        self.used += 1
+        copy = pltpu.make_async_remote_copy(
+            src_ref=src,
+            dst_ref=dst,
+            send_sem=self.send_sems.at[index],
+            recv_sem=self.recv_sems.at[index],
+            device_id=peer,
+            device_id_type=MESH,
+        )
+        copy.start()
+        self.open.append(copy)
+        return copy
+
+    def finish(self):
+        for copy in self.open:
+            copy.wait_send()
+        self.open = []
+
+
+def greet(peers):
+    barrier = pltpu.get_barrier_semaphore()
+    for peer in peers:
+        pl.semaphore_signal(barrier, inc=1, device_id=peer, device_id_type=MESH)
+    return lambda: pl.semaphore_wait(barrier, len(peers))
+
+
+def moe_kernel(
+    normed,
+    ids,
+    gates,
+    w_gate,
+    w_up,
+    w_down,
+    out,
+    tok,
+    stage,
+    tok_a,
+    tok_b,
+    slot_a,
+    slot_b,
+    got_a,
+    got_b,
+    back_a,
+    back_b,
+    acc,
+    hid,
+    w_in,
+    w_out,
+    rank_mask,
+    rank_mask_t,
+    half_send,
+    half_recv,
+    part_send,
+    part_recv,
+    total,
+    z_send,
+    z_plus,
+    z_minus,
+    core_send,
+    core_recv,
+    send_sems,
+    recv_sems,
+    local_sems,
+):
+    x, y, z, core = place()
+    other = 1 - core
+
+    def at(dx=0, dy=0, dz=0, dc=0):
+        return device((x + dx) % 4, (y + dy) % 4, (z + dz) % 8, (core + dc) % 2)
+
+    sibling = at(dc=1)
+    peers = [sibling, at(dz=1), at(dz=7)]
+    for d in (1, 2, 3):
+        for dc in (0, 1):
+            peers.append(at(dx=d, dc=dc))
+            peers.append(at(dy=d, dc=dc))
+    arrived = greet(peers)
+    loads = [
+        pltpu.make_async_copy(w_gate, w_in.at[:, 0:384], local_sems.at[0]),
+        pltpu.make_async_copy(w_up, w_in.at[:, 384:768], local_sems.at[1]),
+        pltpu.make_async_copy(w_down, w_out, local_sems.at[2]),
+    ]
+    for load in loads:
+        load.start()
+
+    lane = lax.broadcasted_iota(jnp.int32, (16, 128), 1)
+    chosen = jnp.zeros((16, 128), F32)
+    weight = jnp.zeros((16, 128), F32)
+    for j in range(TOPK):
+        column = ids[:, j : j + 1]
+        chosen = chosen + jnp.where(lane == column, 1.0, 0.0)
+        weight = weight + jnp.where(lane == column + 64, gates[:, j : j + 1], 0.0)
+    row_i = lax.broadcasted_iota(jnp.int32, (16, 16), 0)
+    col_i = lax.broadcasted_iota(jnp.int32, (16, 16), 1)
+    lower = jnp.where(col_i <= row_i, 1.0, 0.0).astype(BF)
+    rank = jnp.dot(lower, chosen.astype(BF), preferred_element_type=F32)
+    meta = (rank * chosen + weight).astype(BF)
+
+    own_rows = pl.ds(pl.multiple_of(core * 16, 16), 16)
+
+    def columns(k, h):
+        return pl.ds(pl.multiple_of(k * 2048 + h * 1024, 1024), 1024)
+
+    stage[:, 0:1024] = normed[:, columns(other, 0)]
+    stage[:, 1024:1152] = meta
+    stage[:, 1152:2176] = normed[:, columns(other, 1)]
+    tok[own_rows, 0:1024] = normed[:, columns(core, 0)]
+    tok[own_rows, 1024:1152] = meta
+    tok[own_rows, 1152:2176] = normed[:, columns(core, 1)]
+
+    links = Links(send_sems, recv_sems)
+    arrived()
+    links.send(stage, tok.at[own_rows], sibling).wait_recv()
+
+    def rows(dz):
+        return pl.ds(dz * 32, 32)
+
+    dense = {}
+
+    def spread(dz):
+        r = rows(dz)
+        dense["a3", dz] = links.send(tok.at[r, 0:1152], tok_a.at[3, r], at(dx=1))
+        dense["b3", dz] = links.send(tok.at[r, 1024:2176], tok_b.at[3, r], at(dy=1))
+        dense["a1", dz] = links.send(tok.at[r, 0:1152], tok_a.at[1, r], at(dx=3))
+        dense["b1", dz] = links.send(tok.at[r, 1024:2176], tok_b.at[1, r], at(dy=3))
+
+    def relay_up(dz):
+        r = rows(dz)
+        dense["a3", dz].wait_recv()
+        dense["a2", dz] = links.send(tok_a.at[3, r], tok_a.at[2, r], at(dx=1))
+        dense["b3", dz].wait_recv()
+        dense["b2", dz] = links.send(tok_b.at[3, r], tok_b.at[2, r], at(dy=1))
+
+    def relay_down(dz):
+        r = rows(dz)
+        dense["a1", dz].wait_recv()
+        dense["a2", dz] = links.send(tok_a.at[1, r], tok_a.at[2, r], at(dx=3))
+        dense["b1", dz].wait_recv()
+        dense["b2", dz] = links.send(tok_b.at[1, r], tok_b.at[2, r], at(dy=3))
+
+    z_up, z_down = at(dz=1), at(dz=7)
+    up = links.send(tok.at[rows(0)], tok.at[rows(7)], z_up)
+    down = links.send(tok.at[rows(0)], tok.at[rows(1)], z_down)
+    spread(0)
+
+    n = lax.broadcasted_iota(jnp.int32, (8, 48, 256), 1)
+    t = lax.broadcasted_iota(jnp.int32, (8, 48, 256), 2)
+    block = (n * 171) >> 9
+    rank_mask[...] = (
+        jnp.where(block == (t >> 4), n - 3 * block + 1, -1).astype(F32).reshape(384, 256)
+    )
+    r = lax.broadcasted_iota(jnp.int32, (256, 384), 1)
+    t = lax.broadcasted_iota(jnp.int32, (256, 384), 0)
+    n = r - 48 * ((r * 1366) >> 16)
+    block = (n * 171) >> 9
+    rank_mask_t[...] = jnp.where(block == (t >> 4), n - 3 * block + 1, -1).astype(F32)
+
+    q = lax.broadcasted_iota(jnp.int32, (8, 48, 128), 0)
+    lane = lax.broadcasted_iota(jnp.int32, (8, 48, 128), 2)
+    step = q >> 1
+    to_core = (core + (q & 1)) & 1
+    to_y = (y + step) & 3
+    to_x = (x + step) & 3
+    half = z // 4
+    expert_a = 4 * ((x // 2 * 4 + to_y) * 2 + to_core) + 2 * (x % 2) + half
+    expert_b = 4 * (((to_x >> 1) * 4 + y) * 2 + to_core) + 2 * (to_x & 1) + half
+    pick_a = jnp.where(lane == expert_a, 1.0, 0.0).astype(BF).reshape(384, 128)
+    pick_b = jnp.where(lane == expert_b, 1.0, 0.0).astype(BF).reshape(384, 128)
+    pick_aw = jnp.where(lane == expert_a + 64, 1.0, 0.0).astype(BF).reshape(384, 128)
+    pick_bw = jnp.where(lane == expert_b + 64, 1.0, 0.0).astype(BF).reshape(384, 128)
+
+    up.wait_recv()
+    up = links.send(tok.at[rows(7)], tok.at[rows(6)], z_up)
+    down.wait_recv()
+    down = links.send(tok.at[rows(1)], tok.at[rows(2)], z_down)
+    spread(7)
+    spread(1)
+    relay_up(0)
+    up.wait_recv()
+    up = links.send(tok.at[rows(6)], tok.at[rows(5)], z_up)
+    down.wait_recv()
+    down = links.send(tok.at[rows(2)], tok.at[rows(3)], z_down)
+    spread(6)
+    spread(2)
+    relay_up(7)
+    relay_down(1)
+    up.wait_recv()
+    up = links.send(tok.at[pl.ds(5 * 32, 16)], tok.at[pl.ds(4 * 32, 16)], z_up)
+    down.wait_recv()
+    down = links.send(tok.at[pl.ds(3 * 32 + 16, 16)], tok.at[pl.ds(4 * 32 + 16, 16)], z_down)
+    spread(5)
+    spread(3)
+    relay_up(6)
+    relay_down(2)
+    up.wait_recv()
+    down.wait_recv()
+    spread(4)
+    relay_up(5)
+    relay_down(3)
+
+    def tokens(h, d):
+        if d == 0:
+            return tok[:, 0:1024] if h == 0 else tok[:, 1152:2176]
+        return tok_a[d, :, 0:1024] if h == 0 else tok_b[d, :, 128:1152]
+
+    def metas(h, d):
+        if d == 0:
+            return tok[:, 1024:1152]
+        return tok_a[d, :, 1024:1152] if h == 0 else tok_b[d, :, 0:128]
+
+    slot = (slot_a, slot_b)
+    got = (got_a, got_b)
+    back = (back_a, back_b)
+    pick = (pick_a, pick_b)
+    pick_w = (pick_aw, pick_bw)
+
+    def select(h, d):
+        found = lax.dot_general(pick[h], metas(h, d), NT, preferred_element_type=F32)
+        chosen = jnp.where(found == rank_mask[...], 1.0, 0.0).astype(BF)
+        picked = jnp.dot(chosen, tokens(h, d), preferred_element_type=F32)
+        slot[h][SPOS[d]] = picked.astype(BF).reshape(8, 48, 1024)
+
+    def toward(h, d, dc):
+        return at(dx=d, dc=dc) if h else at(dy=d, dc=dc)
+
+    moved = {}
+    kept = {}
+
+    def dispatch(h, part):
+        span = pl.ds(0, 3) if part == 0 else pl.ds(3, 1)
+        for d in (2, 1, 3, 0):
+            for dc in (0, 1):
+                src = slot[h].at[span, d * 2 + dc]
+                dst = got[h].at[((4 - d) % 4) * 2 + dc, span]
+                if d == 0 and dc == 0:
+                    copy = pltpu.make_async_copy(src, dst, local_sems.at[3 + h * 2 + part])
+                    copy.start()
+                    kept[h, part] = copy
+                else:
+                    moved[h, part, d, dc] = links.send(src, dst, toward(h, d, dc))
+
+    select(0, 0)
+    select(1, 0)
+    for dz in range(8):
+        if dz not in (0, 7, 6, 5):
+            dense["a3", dz].wait_recv()
+            dense["b3", dz].wait_recv()
+        if dz not in (1, 2, 3, 4):
+            dense["a1", dz].wait_recv()
+            dense["b1", dz].wait_recv()
+        if dz == 4:
+            relay_down(4)
+    for h in (0, 1):
+        select(h, 1)
+        select(h, 3)
+        dispatch(h, 0)
+    for dz in range(8):
+        dense["a2", dz].wait_recv()
+        dense["b2", dz].wait_recv()
+    for h in (0, 1):
+        select(h, 2)
+        dispatch(h, 1)
+
+    for load in loads:
+        load.wait()
+    acc[...] = jnp.zeros_like(acc)
+    for d in (0, 1, 3, 2):
+        for dc in (0, 1):
+            k = (core + dc) % 2
+            for h in (0, 1):
+                index = d * 2 + dc
+                for part in (0, 1):
+                    if d == 0 and dc == 0:
+                        kept[h, part].wait()
+                    else:
+                        moved[h, part, (4 - d) % 4, dc].wait_recv()
+                term = jnp.dot(
+                    got[h][index].reshape(192, 1024),
+                    w_in[columns(k, h), :],
+                    preferred_element_type=F32,
+                ).reshape(4, 48, 768)
+                if h == 0:
+                    acc[:, SPOS[d]] += term
+                else:
+                    acc[SPOS[d]] += term
+    for i in range(4):
+        gate = acc[i, :, :, 0:384]
+        hid[i] = (gate / (1.0 + jnp.exp(-gate)) * acc[i, :, :, 384:768]).astype(BF)
+
+    returned = {}
+    for d in (2, 1, 3, 0):
+        for dc in (0, 1):
+            k = (core + dc) % 2
+            for h in (0, 1):
+                rows_in = hid[:, SPOS[d]] if h == 0 else hid[SPOS[d]]
+                block_out = (
+                    jnp.dot(
+                        rows_in.reshape(192, 384), w_out[:, columns(k, h)], preferred_element_type=F32
+                    )
+                    .astype(BF)
+                    .reshape(4, 48, 1024)
+                )
+                if d == 0 and dc == 0:
+                    back[h][:, 0] = block_out
+                    continue
+                index = d * 2 + dc
+                target = ((4 - d) % 4) * 2 + dc
+                got[h][index] = block_out
+                for part in (1, 0):
+                    span = pl.ds(0, 3) if part == 0 else pl.ds(3, 1)
+                    returned[h, part, d, dc] = links.send(
+                        got[h].at[index, span], back[h].at[span, target], toward(h, d, dc)
+                    )
+
+    def combine(h, d):
+        info = metas(h, d)
+        found = lax.dot_general(info, pick[h], NT, preferred_element_type=F32)
+        scale = lax.dot_general(info, pick_w[h], NT, preferred_element_type=F32)
+        spread_out = jnp.where(found == rank_mask_t[...], scale, 0.0).astype(BF)
+        return jnp.dot(
+            spread_out, back[h][SPOS[d]].reshape(384, 1024), preferred_element_type=F32
+        )
+
+    def line(h, d):
+        return at(dy=d) if h else at(dx=d)
+
+    halves = {}
+    parts = {}
+    for h in (0, 1):
+        for d in (1, 2, 3, 0):
+            for dc in (0, 1):
+                if d or dc:
+                    returned[h, 1, d, dc].wait_recv()
+        half_send[h] = combine(h, 2).astype(BF)
+        halves[h, 1] = links.send(
+            half_send.at[h, pl.ds(0, 128)], half_recv.at[h, pl.ds(0, 128)], line(h, 1)
+        )
+        halves[h, 3] = links.send(
+            half_send.at[h, pl.ds(128, 128)], half_recv.at[h, pl.ds(128, 128)], line(h, 3)
+        )
+    for h in (0, 1):
+        for d in (1, 2, 3, 0):
+            for dc in (0, 1):
+                if d or dc:
+                    returned[h, 0, d, dc].wait_recv()
+        first = combine(h, 1)
+        third = combine(h, 3)
+        halves[h, 1].wait_recv()
+        part_send[h, 0, 0:128] = (first[0:128] + half_recv[h, 0:128].astype(F32)).astype(BF)
+        part_send[h, 0, 128:256] = first[128:256].astype(BF)
+        parts[h, 1] = links.send(part_send.at[h, 0], part_recv.at[h, 0], line(h, 1))
+        halves[h, 3].wait_recv()
+        part_send[h, 1, 0:128] = third[0:128].astype(BF)
+        part_send[h, 1, 128:256] = (third[128:256] + half_recv[h, 128:256].astype(F32)).astype(BF)
+        parts[h, 3] = links.send(part_send.at[h, 1], part_recv.at[h, 1], line(h, 3))
+    for h in (0, 1):
+        total[:, h * 1024 : (h + 1) * 1024] = combine(h, 0)
+    for h in (0, 1):
+        parts[h, 1].wait_recv()
+        parts[h, 3].wait_recv()
+        total[:, h * 1024 : (h + 1) * 1024] += part_recv[h, 0].astype(F32) + part_recv[
+            h, 1
+        ].astype(F32)
+
+    z_send[4] = total[128:160].astype(BF)
+    up = links.send(z_send.at[4, pl.ds(0, 16)], z_plus.at[3, pl.ds(0, 16)], z_up)
+    down = links.send(z_send.at[4, pl.ds(16, 16)], z_minus.at[3, pl.ds(16, 16)], z_down)
+    for i in (3, 2, 1):
+        rest = 8 - i
+        up.wait_recv()
+        if i == 3:
+            z_send[i, 0:16] = (total[96:112] + z_plus[3, 0:16].astype(F32)).astype(BF)
+            z_send[i, 16:32] = total[112:128].astype(BF)
+        else:
+            z_send[i] = (total[i * 32 : i * 32 + 32] + z_plus[i].astype(F32)).astype(BF)
+        up = links.send(z_send.at[i], z_plus.at[i - 1], z_up)
+        down.wait_recv()
+        if i == 3:
+            z_send[rest, 0:16] = total[160:176].astype(BF)
+            z_send[rest, 16:32] = (total[176:192] + z_minus[3, 16:32].astype(F32)).astype(BF)
+        else:
+            z_send[rest] = (
+                total[rest * 32 : rest * 32 + 32] + z_minus[i].astype(F32)
+            ).astype(BF)
+        down = links.send(z_send.at[rest], z_minus.at[i - 1], z_down)
+    up.wait_recv()
+    down.wait_recv()
+    total[0:32] += z_plus[0].astype(F32) + z_minus[0].astype(F32)
+
+    other_rows = pl.ds(pl.multiple_of(other * 16, 16), 16)
+    core_send[...] = total[other_rows, :]
+    swap = links.send(core_send, core_recv, sibling)
+    out[:, pl.ds(pl.multiple_of(core * 2048, 2048), 2048)] = total[own_rows, :]
+    swap.wait_recv()
+    out[:, pl.ds(pl.multiple_of(other * 2048, 2048), 2048)] = core_recv[...]
+    links.finish()
+
+
+def moe(normed, ids, gates, w_gate, w_up, w_down):
+    vmem = pl.BlockSpec(memory_space=pltpu.VMEM)
+    hbm = pl.BlockSpec(memory_space=pl.ANY)
+    return pl.pallas_call(
+        moe_kernel,
+        out_shape=jax.ShapeDtypeStruct((16, D), F32),
+        in_specs=[vmem, vmem, vmem, hbm, hbm, hbm],
+        out_specs=vmem,
+        scratch_shapes=[
+            pltpu.VMEM((256, 2176), BF),
+            pltpu.VMEM((16, 2176), BF),
+            pltpu.VMEM((4, 256, 1152), BF),
+            pltpu.VMEM((4, 256, 1152), BF),
+            pltpu.VMEM((4, 8, 48, 1024), BF),
+            pltpu.VMEM((4, 8, 48, 1024), BF),
+            pltpu.VMEM((8, 4, 48, 1024), BF),
+            pltpu.VMEM((8, 4, 48, 1024), BF),
+            pltpu.VMEM((4, 8, 48, 1024), BF),
+            pltpu.VMEM((4, 8, 48, 1024), BF),
+            pltpu.VMEM((4, 4, 48, 768), F32),
+            pltpu.VMEM((4, 4, 48, 384), BF),
+            pltpu.VMEM((4096, 768), BF),
+            pltpu.VMEM((384, 4096), BF),
+            pltpu.VMEM((384, 256), F32),
+            pltpu.VMEM((256, 384), F32),
+            pltpu.VMEM((2, 256, 1024), BF),
+            pltpu.VMEM((2, 256, 1024), BF),
+            pltpu.VMEM((2, 2, 256, 1024), BF),
+            pltpu.VMEM((2, 2, 256, 1024), BF),
+            pltpu.VMEM((256, 2048), F32),
+            pltpu.VMEM((8, 32, 2048), BF),
+            pltpu.VMEM((4, 32, 2048), BF),
+            pltpu.VMEM((4, 32, 2048), BF),
+            pltpu.VMEM((16, 2048), F32),
+            pltpu.VMEM((16, 2048), F32),
+            pltpu.SemaphoreType.DMA((MOE_SEMS,)),
+            pltpu.SemaphoreType.DMA((MOE_SEMS,)),
+            pltpu.SemaphoreType.DMA((8,)),
+        ],
+        compiler_params=pltpu.CompilerParams(
+            collective_id=1, has_side_effects=True, vmem_limit_bytes=58 * 2**20
+        ),
+        name="moe",
+    )(normed, ids, gates, w_gate, w_up, w_down)
 
 
 def shards(
@@ -88,55 +562,15 @@
     normed = (hidden_state * lax.rsqrt(square + 1e-06) * norm_gain.astype(jnp.float32)).astype(
         jnp.bfloat16
     )
-    token_count = hidden_state.shape[0]
-    experts = EXP_DEV * expert_count
-    capacity = max(2, 3 * token_count * TOPK // (2 * experts))
-    slot_count = experts * capacity
-    route_list = expert_ids.reshape(token_count * TOPK)
-    expert_match = (route_list[:, None] == jnp.arange(experts, dtype=jnp.int32)[None, :]).astype(
-        jnp.int32
-    )
-    rank_in = jnp.sum(jnp.cumsum(expert_match, 0) * expert_match, 1) - 1
-    slot_index = (route_list % EXP_DEV * expert_count + route_list // EXP_DEV) * capacity + rank_in
-    slot_match = (slot_index[:, None] == jnp.arange(slot_count, dtype=jnp.int32)[None, :]).reshape(
-        token_count, TOPK, slot_count
-    )
-    dispatch_rows = jnp.sum(slot_match.astype(jnp.float32), 1).astype(jnp.bfloat16)
-    combine_rows = jnp.sum(
-        slot_match.astype(jnp.float32) * route_weights.reshape(token_count, TOPK, 1), 1
-    )
-    outgoing = jnp.einsum(
-        "ts,td->sd", dispatch_rows, normed, preferred_element_type=jnp.float32
-    ).astype(jnp.bfloat16)
-    outgoing = outgoing.reshape(EXP_DEV, expert_count, capacity, D)
-    arrived = lax.all_to_all(outgoing, "expert", split_axis=1, concat_axis=1, tiled=True)
-    gate_weight = w_gate[0, 0]
-    up_weight = w_up[0, 0]
-    down_weight = w_down[0, 0]
-    slices = seq_count // EXP_DEV
-    spread = jnp.repeat(arrived, slices, axis=0)
-    rows_in = lax.all_to_all(spread, "seq", split_axis=0, concat_axis=0, tiled=True)
-    row_block = rows_in.reshape(-1, D)
-    gate_proj = jnp.dot(row_block, gate_weight, preferred_element_type=jnp.float32)
-    up_proj = jnp.dot(row_block, up_weight, preferred_element_type=jnp.float32)
-    hidden = (jax.nn.silu(gate_proj) * up_proj).astype(jnp.bfloat16)
-    partial_value = (
-        jnp.dot(hidden, down_weight, preferred_element_type=jnp.float32)
-        .astype(jnp.bfloat16)
-        .reshape(seq_count, expert_count, capacity, D)
-    )
-    returned_parts = lax.all_to_all(partial_value, "seq", split_axis=0, concat_axis=0, tiled=True)
-    expert_sum = jnp.sum(
-        returned_parts.reshape(EXP_DEV, slices, expert_count, capacity, D), 1, dtype=jnp.float32
-    )
-    outputs = expert_sum.astype(jnp.bfloat16)
-    returned = lax.all_to_all(outputs, "expert", split_axis=1, concat_axis=1, tiled=True)
-    expert_mix = jnp.dot(
-        combine_rows,
-        returned.reshape(slot_count, D).astype(jnp.float32),
-        precision=lax.Precision.HIGHEST,
-    )
-    return (hidden_state + expert_mix).astype(jnp.bfloat16).reshape(residual_in.shape)
+    mixed = moe(
+        normed,
+        expert_ids.reshape(16, TOPK),
+        route_weights.reshape(16, TOPK),
+        w_gate[0, 0],
+        w_up[0, 0],
+        w_down[0, 0],
+    )
+    return (hidden_state + mixed).astype(jnp.bfloat16).reshape(residual_in.shape)
 
 
 def solution(mesh):

time: 763 us -> 488 us (0.64)
  blocking collectives: 346 us -> 0 us
  Pallas kernels: 0 us -> 154 us
  local copies, waits for them, and re-layouts: 72.3 us -> 8.51 us
  matrix products: 37.7 us -> 15.4 us
    all_to_all x4 -> x0, blocking collectives: 346 us -> none  [the longest x1 143 us: shards(): lax.all_to_all(spread, 'seq', split_axis=0, concat_axis=0, tiled=True)]
    pallas_call x0 -> x1, Pallas kernels: none -> 154 us  [moe(): pl.pallas_call(moe_kernel, out_shape=jax.ShapeDtypeStruct((16, D), F32),...]
    reshape x7 -> x1, local copies, waits for them, and re-layouts: 48.3 us -> 0.76 us  [shards(): (hidden_state + mixed).astype(jnp.bfloat16).reshape(residual_in.shape)]
    dot_general x5 -> x0, matrix products: 20.8 us -> none  [the longest x1 6.57 us: shards(): jnp.dot(row_block, gate_weight, preferred_element_type=jnp.float32)]
    all_to_all x3 -> x0, local copies, waits for them, and re-layouts: 15.1 us -> none  [the longest x1 11.5 us: shards(): lax.all_to_all(spread, 'seq', split_axis=0, concat_axis=0, tiled=True)]
where the time goes in v1:
time: 488 us; the launch traced here: 486 us
  waiting for transfers between devices  288 us (59%)
  Pallas kernels  154 us (32%)
  matrix products  15.4 us (3%)
  between operations  13.3 us (3%)
  local copies, waits for them, and re-layouts  8.51 us (2%)
  other arithmetic  5.78 us (1%)
    pallas_call x1, Pallas kernels, moe(): pl.pallas_call(moe_kernel, out_shape=jax.ShapeDtypeStruct((16, D), F32),...  154 us
    reduce_scatter x1, waiting for transfers between devices, shards(): lax.psum_scatter(term_rows.astype(jnp.bfloat16), 'expert', scatter_dimens...  85.6 us
    all_gather x1, waiting for transfers between devices, shards(): lax.all_gather(out_weight, 'seq', axis=1, tiled=True)  83 us
    all_gather x1, waiting for transfers between devices, shards(): piece_values = lax.all_gather(own_values, 'seq', axis=0, tiled=True)  59.9 us
    all_gather x1, waiting for transfers between devices, shards(): piece_keys = lax.all_gather(own_keys, 'seq', axis=0, tiled=True)  58.9 us
  transfers between devices with their start and end apart: 4, of which 4 were waited for; matrix products, arithmetic and copies ran while one was open for 3% of the time, Pallas kernels for 0%

profile of v1, /device:TPU:1, one launch (start us, length us, event | category | flops | bytes accessed | tf_op | source)
XLA Modules:
  0.0 485.6 jit_solution(2223421251884340631)
XLA Ops:
  6.5 0.9 copy-done
  7.5 0.6 copy.30
  8.3 0.9 constant_dynamic-slice_fusion
  9.1 0.6 copy.31
  9.9 0.7 all-gather.8.cloned.1.call-update
  10.6 1.1 reshape.53
  11.7 0.9 fusion.21
  12.7 0.2 iota_compare_fusion
  12.9 58.9 %all-gather.4.cloned.1.call-done = bf16[2048,2,128]{2,0,1:T(8,128)(2,1)} async-done(((bf16[128,2,128]{2,0,1:T(8,128)(2,1)}), bf16[2048,2,128]{2,0,1:T(8,128)(2,1)}) %all-gather.4.cloned.1.call-update) | async-done | bytes 1048592 | tf_op jit(solution)/shard_map/all_gather | solution.py:532
  71.8 2.6 fusion
  74.5 3.2 copy-done.1
  77.7 1.7 convert_reduce_fusion
  79.4 1.0 fusion.1
  80.4 59.9 %all-gather.6.cloned.1.call-done = bf16[2048,2,128]{2,0,1:T(8,128)(2,1)} async-done(((bf16[128,2,128]{2,0,1:T(8,128)(2,1)}), bf16[2048,2,128]{2,0,1:T(8,128)(2,1)}) %all-gather.6.cloned.1.call-update) | async-done | bytes 1048592 | tf_op jit(solution)/shard_map/all_gather | solution.py:533
  140.4 6.1 %fusion.4 = bf16[128,2,4,128]{3,0,2,1:T(8,128)(2,1)S(1)} fusion(f32[128,2,4,128]{3,0,2,1:T(8,128)S(1)} %fusion.1, bf16[2048,2,128]{2,0,1:T(8,128)(2,1)} %all-gather.6.cloned.1.call-done, f32[128,2,4]{0,2,1:T(4,128)S(1)} %get-tuple-element.5, f32[2,2048,128,4]{2,1,3,0:T(8,128)} %copy-done.1, f32[2,4,128]{2,1,0:T(4,128)S(1)} %max.18, ...), kind=kOutput, calls=%fused_computation.10 | convolution fusion | flops 545652736 | bytes 10493952 | tf_op jit(solution)/shard_map/bhij,jbd->bhid/dot_general | solution.py:546
  146.5 0.2 copy.24
  146.7 83.0 %all-gather.8.cloned.1.call-done = bf16[512,4096]{1,0:T(8,128)(2,1)} async-done(((bf16[512,256]{1,0:T(8,128)(2,1)}), bf16[512,4096]{1,0:T(8,128)(2,1)}) %all-gather.8.cloned.1.call-update) | async-done | bytes 4194320 | tf_op jit(solution)/shard_map/all_gather | solution.py:554
  229.7 4.8 convolution_convert_fusion
  234.6 85.6 %reduce-scatter.2.cloned.1.call-done = bf16[16,4096]{1,0:T(8,128)(2,1)} async-done(((bf16[256,4096]{1,0:T(8,128)(2,1)}), bf16[16,4096]{1,0:T(8,128)(2,1)}) %reduce-scatter.2.cloned.1.call-update) | async-done | bytes 131088 | tf_op jit(solution)/shard_map/reduce_scatter | solution.py:557
  320.2 1.1 multiply_reduce_fusion
  321.4 1.7 multiply_convert_fusion.normed
  323.0 154.3 %moe.1 = f32[16,4096]{1,0:T(8,128)} custom-call(bf16[16,4096]{1,0:T(8,128)(2,1)} %multiply_convert_fusion.normed, s32[16,8]{1,0:T(8,128)} %bitcast.74, f32[16,8]{1,0:T(8,128)} %bitcast.75, bf16[4096,384]{1,0:T(8,128)(2,1)} %bitcast.70, bf16[4096,384]{1,0:T(8,128)(2,1)} %bitcast.71, bf16[384,4096]{1,0:T(8,128)(2,1)} %bitcast.72), custom_call_target="tpu_custom_call" | custom-call | tf_op jit(solution)/shard_map/moe/pallas_call | solution.py:446
  477.3 1.0 add_convert_fusion
  478.3 0.8 reshape.57
  (23 shorter events, 0.4 us)
Async XLA Ops:
  6.5 1.0 copy-start
  6.5 65.3 %all-gather.4.cloned.1.call-start = ((), (), s32[]{:S(2)}) async-start(), calls=%async_computation.1 | async-start | bytes 1114112 | tf_op jit(solution)/shard_map/all_gather | solution.py:532
  8.2 132.2 %all-gather.6.cloned.1.call-start = ((), (), s32[]{:S(2)}) async-start(), calls=%async_computation.2 | async-start | bytes 1114112 | tf_op jit(solution)/shard_map/all_gather | solution.py:533
  9.8 219.9 %all-gather.8.cloned.1.call-start = ((), (), s32[]{:S(2)}) async-start(), calls=%async_computation.3 | async-start | bytes 4456448 | tf_op jit(solution)/shard_map/all_gather | solution.py:554
  10.5 309.7 %reduce-scatter.2.cloned.1.call-start = ((), (), s32[]{:S(2)}) async-start(), calls=%async_computation.4 | async-start | bytes 2228224 | tf_op jit(solution)/shard_map/reduce_scatter | solution.py:557
  74.4 3.2 copy-start.1
  146.4 88.1 %copy-start.3 = (bf16[8,2,4096]{2,1,0:T(2,128)(2,1)S(1)}, bf16[8,2,4096]{2,1,0:T(2,128)(2,1)}, u32[]{:S(2)}) copy-start(bf16[8,2,4096]{2,1,0:T(2,128)(2,1)} %param.19) | copy-start | bytes 393220
  146.5 88.1 %copy-start.4 = (bf16[4096]{0:T(1024)(128)(2,1)S(1)}, bf16[4096]{0:T(1024)(128)(2,1)}, u32[]{:S(2)}) copy-start(bf16[4096]{0:T(1024)(128)(2,1)} %param.20) | copy-start | bytes 24580
  320.2 157.1 %copy-start.2 = (bf16[16,4096]{1,0:T(8,128)(2,1)S(1)}, bf16[16,4096]{1,0:T(8,128)(2,1)}, u32[]{:S(2)}) copy-start(bf16[16,4096]{1,0:T(8,128)(2,1)} %reduce-scatter.2.cloned.1.call-done) | copy-start | bytes 393220
Sparse Core Ops, SparseCore 0:
  9.2 62.6 all-gather.3
  73.6 66.6 all-gather.5
  142.1 87.5 all-gather.7
  234.7 85.5 reduce-scatter.1

commit v2 on v1

--- a/solution.py
+++ b/solution.py
@@ -9,10 +9,7 @@
 
 D = 4096
 HD = 128
-KV = 4
-EXP_DEV = 4
 TOPK = 8
-
 
 MESH = pl.DeviceIdType.MESH
 BF = jnp.bfloat16
@@ -486,6 +483,327 @@
     )(normed, ids, gates, w_gate, w_up, w_down)
 
 
+ATT_SEMS = 96
+
+
+def attn_kernel(
+    queries,
+    keys,
+    values,
+    prefix_keys,
+    prefix_values,
+    out_weight,
+    residual,
+    gain,
+    hidden,
+    normed,
+    kv,
+    wts,
+    qs,
+    pre_k,
+    pre_v,
+    scores,
+    pre_scores,
+    top,
+    summed,
+    weighted,
+    att,
+    att_bf,
+    own_term,
+    core_send,
+    core_recv,
+    y_send,
+    y_recv,
+    x_send,
+    x_recv,
+    send_sems,
+    recv_sems,
+    local_sems,
+):
+    x, y, z, core = place()
+    other = 1 - core
+    x_lo = x % 2
+    kv_head = (lax.axis_index("expert")) // 4
+
+    def at(dx=0, dy=0, dz=0, dc=0):
+        return device((x + dx) % 4, (y + dy) % 4, (z + dz) % 8, (core + dc) % 2)
+
+    sibling = at(dc=1)
+    partner = device(x + 1 - 2 * x_lo, y, z, core)
+    z_up, z_down = at(dz=1), at(dz=7)
+    peers = [sibling, z_up, z_down]
+    for d in (1, 2, 3):
+        peers.append(at(dx=d))
+        peers.append(at(dy=d))
+    arrived = greet(peers)
+    load = pltpu.make_async_copy(out_weight, wts.at[0], local_sems.at[0])
+    load.start()
+    for b in range(2):
+        col = pl.ds(pl.multiple_of(b * 512 + kv_head * 128, 128), 128)
+        kv[core, 0, :, b * 128 : (b + 1) * 128] = jnp.where(
+            core == 0, keys[:, col].astype(F32), values[:, col].astype(F32)
+        ).astype(BF)
+    links = Links(send_sems, recv_sems)
+    arrived()
+
+    across = {}
+    shared = {}
+
+    def hand_on(dz):
+        shared[0, dz] = links.send(kv.at[core, dz], kv.at[core, dz], sibling)
+        across[dz] = links.send(kv.at[core, dz], kv.at[core, 8 + dz], partner)
+
+    def hand_over(dz):
+        across[dz].wait_recv()
+        shared[1, dz] = links.send(kv.at[core, 8 + dz], kv.at[core, 8 + dz], sibling)
+
+    low, high = pl.ds(0, 64), pl.ds(64, 64)
+    up = links.send(kv.at[core, 0], kv.at[core, 7], z_up)
+    down = links.send(kv.at[core, 0], kv.at[core, 1], z_down)
+    hand_on(0)
+    load.wait()
+    w_up = links.send(wts.at[0], wts.at[7], z_up)
+    w_down = links.send(wts.at[0], wts.at[1], z_down)
+
+    for b in range(2):
+        for h in range(4):
+            qs[b, h * 128 : (h + 1) * 128, :] = queries[:, b * 512 + h * 128 : b * 512 + h * 128 + 128]
+    head_cols = pl.ds(pl.multiple_of(kv_head * 128, 128), 128)
+    pre_k[0:64] = prefix_keys[:, head_cols]
+    pre_k[64:128] = jnp.zeros((64, 128), BF)
+    pre_v[0:64] = prefix_values[:, head_cols]
+    pre_v[64:128] = jnp.zeros((64, 128), BF)
+
+    up.wait_recv()
+    up = links.send(kv.at[core, 7], kv.at[core, 6], z_up)
+    down.wait_recv()
+    down = links.send(kv.at[core, 1], kv.at[core, 2], z_down)
+    hand_on(7)
+    hand_on(1)
+    hand_over(0)
+    up.wait_recv()
+    up = links.send(kv.at[core, 6], kv.at[core, 5], z_up)
+    down.wait_recv()
+    down = links.send(kv.at[core, 2], kv.at[core, 3], z_down)
+    hand_on(6)
+    hand_on(2)
+    hand_over(7)
+    hand_over(1)
+    up.wait_recv()
+    up = links.send(kv.at[core, 5, low], kv.at[core, 4, low], z_up)
+    down.wait_recv()
+    down = links.send(kv.at[core, 3, high], kv.at[core, 4, high], z_down)
+    hand_on(5)
+    hand_on(3)
+    hand_over(6)
+    hand_over(2)
+    up.wait_recv()
+    down.wait_recv()
+    hand_on(4)
+    w_up.wait_recv()
+    w_up = links.send(wts.at[7], wts.at[6], z_up)
+    w_down.wait_recv()
+    w_down = links.send(wts.at[1], wts.at[2], z_down)
+    hand_over(5)
+    hand_over(3)
+    hand_over(4)
+    for dz in range(8):
+        shared[0, dz].wait_recv()
+        shared[1, dz].wait_recv()
+
+    scale = 1.0 / math.sqrt(HD)
+    gap = lax.broadcasted_iota(jnp.int32, (4, 128, 128), 2) - lax.broadcasted_iota(
+        jnp.int32, (4, 128, 128), 1
+    )
+    gap = gap.reshape(512, 128)
+    pre_lane = lax.broadcasted_iota(jnp.int32, (512, 128), 1)
+
+    def attend(b):
+        cols = slice(b * 128, (b + 1) * 128)
+        first = lax.dot_general(qs[b], pre_k[...], NT, preferred_element_type=F32) * scale
+        first = jnp.where(pre_lane < 64, first, -1e30)
+        pre_scores[...] = first
+        top[...] = first
+
+        def score(c, carry):
+            block = lax.dot_general(
+                qs[b],
+                kv[0, pl.ds(2 * c, 2), :, cols].reshape(256, 128),
+                NT,
+                preferred_element_type=F32,
+            )
+            best = top[...]
+            for r in range(2):
+                theirs = ((x_lo + c // 4) % 2) * 8 + (z + 2 * c + r) % 8
+                ahead = (x_lo * 8 + z - theirs) * 128
+                part = jnp.where(gap <= ahead, block[:, r * 128 : (r + 1) * 128] * scale, -1e30)
+                scores[c, :, r * 128 : (r + 1) * 128] = part
+                best = jnp.maximum(best, part)
+            top[...] = best
+            return carry
+
+        lax.fori_loop(0, 8, score, 0)
+        top[...] = jnp.broadcast_to(jnp.max(top[...], -1, keepdims=True), (512, 128))
+        probs = jnp.exp(pre_scores[...] - top[...]).astype(BF)
+        summed[...] = probs.astype(F32)
+        weighted[...] = jnp.dot(probs, pre_v[...], preferred_element_type=F32)
+
+        def mix(c, carry):
+            peak = top[...]
+            left = jnp.exp(scores[c, :, 0:128] - peak).astype(BF)
+            right = jnp.exp(scores[c, :, 128:256] - peak).astype(BF)
+            summed[...] += left.astype(F32) + right.astype(F32)
+            weighted[...] += jnp.dot(
+                jnp.concatenate([left, right], axis=1),
+                kv[1, pl.ds(2 * c, 2), :, cols].reshape(256, 128),
+                preferred_element_type=F32,
+            )
+            return carry
+
+        lax.fori_loop(0, 8, mix, 0)
+        result = weighted[...] / jnp.sum(summed[...], -1, keepdims=True)
+        for h in range(4):
+            for e in range(16):
+                start = h * 128 + e * 8
+                att[e % 2, (e // 2) % 4, e // 8, b, :, h * 128 : (h + 1) * 128] = result[
+                    start : start + 8
+                ]
+
+    attend(0)
+    w_up.wait_recv()
+    w_up = links.send(wts.at[6], wts.at[5], z_up)
+    w_down.wait_recv()
+    w_down = links.send(wts.at[2], wts.at[3], z_down)
+    attend(1)
+    att_bf[0] = att[...].reshape(256, 512).astype(BF)
+    swap = links.send(att_bf.at[0], att_bf.at[1], partner)
+    w_up.wait_recv()
+    w_up = links.send(wts.at[5, pl.ds(0, 256)], wts.at[4, pl.ds(0, 256)], z_up)
+    w_down.wait_recv()
+    w_down = links.send(wts.at[3, pl.ds(256, 256)], wts.at[4, pl.ds(256, 256)], z_down)
+    swap.wait_recv()
+
+    def half(c):
+        rows = pl.ds(pl.multiple_of(c * 128, 128), 128)
+        return att_bf[:, rows, :].reshape(256, 512)
+
+    chunks = ((0, 7), (1, 6), (2, 5), (3, 4))
+    core_moves, y_moves, x_moves = {}, {}, {}
+
+    def project(j):
+        if j == 3:
+            w_up.wait_recv()
+            w_down.wait_recv()
+        for i, dz in enumerate(chunks[j]):
+            cols = slice(i * 256, (i + 1) * 256)
+            core_send[j, :, :, :, :, cols] = (
+                jnp.dot(half(other), wts[dz], preferred_element_type=F32)
+                .astype(BF)
+                .reshape(2, 4, 2, 16, 256)
+            )
+        core_moves[j] = links.send(core_send.at[j], core_recv.at[j], sibling)
+        for i, dz in enumerate(chunks[j]):
+            cols = slice(i * 256, (i + 1) * 256)
+            own_term[j, :, :, :, :, cols] = jnp.dot(
+                half(core), wts[dz], preferred_element_type=F32
+            ).reshape(2, 4, 2, 16, 256)
+
+    def along_y(j):
+        core_moves[j].wait_recv()
+        both = own_term[j] + core_recv[j].astype(F32)
+        own_term[j] = both
+        y_send[j] = both.astype(BF)
+        for d in (2, 1, 3):
+            y_moves[j, d] = links.send(
+                y_send.at[j, :, (y + d) % 4], y_recv.at[j, (4 - d) % 4], at(dy=d)
+            )
+
+    def along_x(j):
+        own = own_term[j, :, y]
+        for d in (1, 2, 3):
+            y_moves[j, d].wait_recv()
+        for d in (1, 2, 3):
+            own = own + y_recv[j, d].astype(F32)
+        own_term[j, :, y] = own
+        x_send[j] = own.astype(BF)
+        for d in (2, 1, 3):
+            x_moves[j, d] = links.send(
+                x_send.at[j, d % 2, ((x + d) % 4) // 2], x_recv.at[j, (4 - d) % 4], at(dx=d)
+            )
+
+    square = jnp.zeros((16, 128), F32)
+
+    def join(j, square):
+        for d in (1, 2, 3):
+            x_moves[j, d].wait_recv()
+        mine = own_term[j, 0, y, x // 2] + x_recv[j, 2].astype(F32)
+        theirs = x_recv[j, 1].astype(F32) + x_recv[j, 3].astype(F32)
+        for i, dz in enumerate(chunks[j]):
+            for side, part in ((x_lo, mine), (1 - x_lo, theirs)):
+                where = pl.ds(pl.multiple_of((side * 8 + (z + dz) % 8) * 256, 256), 256)
+                value = residual[:, where].astype(F32) + part[:, i * 256 : (i + 1) * 256]
+                hidden[:, where] = value
+                value = value * value
+                square = square + value[:, 0:128] + value[:, 128:256]
+        return square
+
+    project(0)
+    project(1)
+    along_y(0)
+    project(2)
+    along_y(1)
+    project(3)
+    along_y(2)
+    along_x(0)
+    along_y(3)
+    for j in (1, 2, 3):
+        along_x(j)
+    for j in range(4):
+        square = join(j, square)
+    mean = jnp.sum(square, -1, keepdims=True) * (1.0 / D)
+    normed[...] = (hidden[...] * lax.rsqrt(mean + 1e-06) * gain[...].astype(F32)).astype(BF)
+    links.finish()
+
+
+def attention(queries, keys, values, prefix_keys, prefix_values, out_weight, residual, gain):
+    vmem = pl.BlockSpec(memory_space=pltpu.VMEM)
+    hbm = pl.BlockSpec(memory_space=pl.ANY)
+    return pl.pallas_call(
+        attn_kernel,
+        out_shape=(jax.ShapeDtypeStruct((16, D), F32), jax.ShapeDtypeStruct((16, D), BF)),
+        in_specs=[vmem, vmem, vmem, vmem, vmem, hbm, vmem, vmem],
+        out_specs=(vmem, vmem),
+        scratch_shapes=[
+            pltpu.VMEM((2, 16, 128, 256), BF),
+            pltpu.VMEM((8, 512, 256), BF),
+            pltpu.VMEM((2, 512, 128), BF),
+            pltpu.VMEM((128, 128), BF),
+            pltpu.VMEM((128, 128), BF),
+            pltpu.VMEM((8, 512, 256), F32),
+            pltpu.VMEM((512, 128), F32),
+            pltpu.VMEM((512, 128), F32),
+            pltpu.VMEM((512, 128), F32),
+            pltpu.VMEM((512, 128), F32),
+            pltpu.VMEM((2, 4, 2, 2, 8, 512), F32),
+            pltpu.VMEM((2, 256, 512), BF),
+            pltpu.VMEM((4, 2, 4, 2, 16, 512), F32),
+            pltpu.VMEM((4, 2, 4, 2, 16, 512), BF),
+            pltpu.VMEM((4, 2, 4, 2, 16, 512), BF),
+            pltpu.VMEM((4, 2, 4, 2, 16, 512), BF),
+            pltpu.VMEM((4, 4, 2, 2, 16, 512), BF),
+            pltpu.VMEM((4, 2, 2, 16, 512), BF),
+            pltpu.VMEM((4, 4, 16, 512), BF),
+            pltpu.SemaphoreType.DMA((ATT_SEMS,)),
+            pltpu.SemaphoreType.DMA((ATT_SEMS,)),
+            pltpu.SemaphoreType.DMA((1,)),
+        ],
+        compiler_params=pltpu.CompilerParams(
+            collective_id=2, has_side_effects=True, vmem_limit_bytes=48 * 2**20
+        ),
+        name="attention",
+    )(queries, keys, values, prefix_keys, prefix_values, out_weight, residual, gain)
+
+
 def shards(
     queries,
     keys,
@@ -501,76 +819,29 @@
     w_up,
     w_down,
 ):
-    seq_count = lax.axis_size("seq")
-    expert_count = lax.axis_size("expert")
-    seq_place = lax.axis_index("seq")
-    expert_place = lax.axis_index("expert")
-    block_len, seq_num, query_width = queries.shape
-    heads_local = query_width // HD
-    head_group = heads_local * expert_count // KV
-    shared_head = expert_place * heads_local // head_group
-    own_keys = lax.dynamic_slice_in_dim(keys, shared_head * HD, HD, 2)
-    own_values = lax.dynamic_slice_in_dim(values, shared_head * HD, HD, 2)
-    prefix_key = lax.dynamic_slice_in_dim(prefix_keys, shared_head * HD, HD, 1)
-    prefix_value = lax.dynamic_slice_in_dim(prefix_values, shared_head * HD, HD, 1)
-    score_scale = 1.0 / math.sqrt(HD)
-    grouped_q = queries.reshape(block_len, seq_num, heads_local, HD)
-    prefix_scores = (
-        jnp.einsum("ibhd,pd->bhip", grouped_q, prefix_key, preferred_element_type=jnp.float32)
-        * score_scale
-    )
-    prefix_top = jnp.max(prefix_scores, -1)
-    prefix_weights = jnp.exp(prefix_scores - prefix_top[..., None]).astype(jnp.bfloat16)
-    prefix_total = jnp.sum(prefix_weights, -1, dtype=jnp.float32)
-    prefix_sum = jnp.einsum(
-        "bhip,pd->bhid", prefix_weights, prefix_value, preferred_element_type=jnp.float32
-    )
-    query_places = seq_place * block_len + jnp.arange(block_len, dtype=jnp.int32)
-    row_top = prefix_top
-    row_total = prefix_total
-    weighted = prefix_sum
-    piece_keys = lax.all_gather(own_keys, "seq", axis=0, tiled=True)
-    piece_values = lax.all_gather(own_values, "seq", axis=0, tiled=True)
-    key_count = piece_keys.shape[0]
-    scores = (
-        jnp.einsum("ibhd,jbd->bhij", grouped_q, piece_keys, preferred_element_type=jnp.float32)
-        * score_scale
-    )
-    key_places = jnp.arange(key_count, dtype=jnp.int32)
-    allowed = key_places[None, :] <= query_places[:, None]
-    scores = jnp.where(allowed, scores, -1e30)
-    new_top = jnp.maximum(row_top, jnp.max(scores, -1))
-    probabilities = jnp.exp(scores - new_top[..., None]).astype(jnp.bfloat16)
-    shrink = jnp.exp(row_top - new_top)
-    row_total = row_total * shrink + jnp.sum(probabilities, -1, dtype=jnp.float32)
-    weighted = weighted * shrink[..., None] + jnp.einsum(
-        "bhij,jbd->bhid", probabilities, piece_values, preferred_element_type=jnp.float32
-    )
-    row_top, row_total, weighted = (new_top, row_total, weighted)
-    attended = (weighted / row_total[..., None]).astype(jnp.bfloat16)
-    attended = jnp.transpose(attended, (2, 0, 1, 3)).reshape(block_len * seq_num, heads_local * HD)
-    term_rows = jnp.dot(
-        attended,
-        lax.all_gather(out_weight, "seq", axis=1, tiled=True),
-        preferred_element_type=jnp.float32,
-    )
-    summed = lax.psum_scatter(
-        term_rows.astype(jnp.bfloat16), "expert", scatter_dimension=0, tiled=True
-    ).astype(jnp.float32)
-    hidden_state = residual_in.reshape(-1, D).astype(jnp.float32) + summed
-    square = jnp.mean(hidden_state * hidden_state, -1, keepdims=True)
-    normed = (hidden_state * lax.rsqrt(square + 1e-06) * norm_gain.astype(jnp.float32)).astype(
-        jnp.bfloat16
+    def by_sequence(array):
+        return jnp.transpose(array, (1, 0, 2)).reshape(16, array.shape[-1])
+
+    hidden_state, normed = attention(
+        queries.reshape(128, 1024),
+        keys.reshape(128, 1024),
+        values.reshape(128, 1024),
+        prefix_keys,
+        prefix_values,
+        out_weight,
+        by_sequence(residual_in),
+        norm_gain.reshape(1, D),
     )
     mixed = moe(
         normed,
-        expert_ids.reshape(16, TOPK),
-        route_weights.reshape(16, TOPK),
+        by_sequence(expert_ids),
+        by_sequence(route_weights),
         w_gate[0, 0],
         w_up[0, 0],
         w_down[0, 0],
     )
-    return (hidden_state + mixed).astype(jnp.bfloat16).reshape(residual_in.shape)
+    mixed = (hidden_state + mixed).astype(BF)
+    return jnp.transpose(mixed.reshape(2, 8, D), (1, 0, 2))
 
 
 def solution(mesh):

time: 488 us -> 230 us (0.47)
  waiting for transfers between devices: 288 us -> 0 us
  Pallas kernels: 154 us -> 218 us
  matrix products: 15.4 us -> 0 us
  between operations: 13.3 us -> 0.07 us
    all_gather x3 -> x0, waiting for transfers between devices: 202 us -> none  [the longest x1 83 us: shards(): lax.all_gather(out_weight, 'seq', axis=1, tiled=True)]
    reduce_scatter x1 -> x0, waiting for transfers between devices: 85.6 us -> none  [shards(): lax.psum_scatter(term_rows.astype(jnp.bfloat16), 'expert', scatter_dimens...]
    pallas_call x0 -> x1, Pallas kernels: none -> 66.2 us  [attention(): pl.pallas_call(attn_kernel, out_shape=(jax.ShapeDtypeStruct((16, D), F32)...]
    dot_general x5 -> x0, matrix products: 15.4 us -> none  [the longest x1 6.07 us: shards(): jnp.einsum('bhij,jbd->bhid', probabilities, piece_values, preferred_eleme...]
  transfers between devices with their start and end apart: 4 -> 0, of which waited for: 4 -> 0; matrix products, arithmetic and copies ran while one was open for 3% -> 0% of each run, Pallas kernels for 0% -> 0%
where the time goes in v2:
time: 230 us; the launch traced here: 229 us
  Pallas kernels  218 us (95%)
  local copies, waits for them, and re-layouts  9.93 us (4%)
    pallas_call x1, Pallas kernels, moe(): pl.pallas_call(moe_kernel, out_shape=jax.ShapeDtypeStruct((16, D), F32),...  152 us
    pallas_call x1, Pallas kernels, attention(): pl.pallas_call(attn_kernel, out_shape=(jax.ShapeDtypeStruct((16, D), F32)...  66.2 us
    unnamed x15, local copies, waits for them, and re-layouts  6.25 us

profile of v2, /device:TPU:1, one launch (start us, length us, event | category | flops | bytes accessed | tf_op | source)
XLA Modules:
  0.0 229.2 jit_solution(4900446734636728362)
XLA Ops:
  0.0 0.0 copy-start.4
  0.0 0.0 copy-start.5
  0.0 1.0 copy.24
  1.0 1.0 copy.25
  2.0 1.0 copy.26
  3.0 1.0 copy.32
  4.0 0.7 reshape.28.gain
  4.7 0.0 copy-start
  4.7 0.9 copy-done
  5.6 0.0 copy-start.2
  5.6 0.8 copy-done.2
  6.5 0.0 copy-start.3
  6.5 0.8 copy-done.3
  7.3 66.2 %attention.1 = (f32[16,4096]{1,0:T(8,128)S(1)}, bf16[16,4096]{1,0:T(8,128)(2,1)S(1)}) custom-call(bf16[128,1024]{1,0:T(8,128)(2,1)S(1)} %bitcast.26, bf16[128,1024]{1,0:T(8,128)(2,1)S(1)} %bitcast.27, bf16[128,1024]{1,0:T(8,128)(2,1)S(1)} %bitcast.28, bf16[64,512]{1,0:T(8,128)(2,1)S(1)} %copy-done.2, bf16[64,512]{1,0:T(8,128)(2,1)S(1)} %copy-done.3, ...), custom_call_target="tpu_custom_call" | custom-call | tf_op jit(solution)/shard_map/attention/pallas_call | solution.py:771
  73.5 0.0 copy-start.1
  73.5 0.6 copy-done.1
  74.2 0.0 copy-done.4
  74.2 0.6 copy.33
  74.8 0.0 copy-done.5
  74.8 0.6 copy.34
  75.4 152.0 %moe.1 = f32[16,4096]{1,0:T(8,128)} custom-call(bf16[16,4096]{1,0:T(8,128)(2,1)} %copy-done.1, s32[16,8]{1,0:T(8,128)} %bitcast.38, f32[16,8]{1,0:T(8,128)} %bitcast.37, bf16[4096,384]{1,0:T(8,128)(2,1)} %bitcast.30, bf16[4096,384]{1,0:T(8,128)(2,1)} %bitcast.31, bf16[384,4096]{1,0:T(8,128)(2,1)} %bitcast.32), custom_call_target="tpu_custom_call" | custom-call | tf_op jit(solution)/shard_map/moe/pallas_call | solution.py:443
  227.4 1.0 fusion
  228.4 0.8 copy.31
Async XLA Ops:
  0.0 74.2 %copy-start.4 = (f32[8,2,8]{2,1,0:T(2,128)S(1)}, f32[8,2,8]{2,1,0:T(2,128)}, u32[]{:S(2)}) copy-start(f32[8,2,8]{2,1,0:T(2,128)} %param.22) | copy-start | bytes 1540
  0.0 74.8 %copy-start.5 = (s32[8,2,8]{2,1,0:T(2,128)S(1)}, s32[8,2,8]{2,1,0:T(2,128)}, u32[]{:S(2)}) copy-start(s32[8,2,8]{2,1,0:T(2,128)} %param.21) | copy-start | bytes 1540
  4.7 1.0 copy-start
  5.6 0.8 copy-start.2
  6.5 0.8 copy-start.3
  73.5 0.7 copy-start.1

commit v3 on v2

v3 whole, which is shorter than its diff:
```python
import math

import jax
import jax.numpy as jnp
from jax import lax
from jax.experimental import pallas as pl
from jax.experimental.pallas import tpu as pltpu
from jax.sharding import PartitionSpec as P

D = 4096
HD = 128
TOPK = 8

MESH = pl.DeviceIdType.MESH
BF = jnp.bfloat16
F32 = jnp.float32
NT = (((1,), (1,)), ((), ()))
ORDER = (0, 1, 3, 2)
SPOS = {0: 0, 1: 1, 3: 2, 2: 3}
MOE_SEMS = 104
FAR = (1, 2, 3)


def place():
    s = lax.axis_index("seq")
    e = lax.axis_index("expert")
    return (e // 8) * 2 + s // 8, (e // 2) % 4, s % 8, e % 2


def device(x, y, z, c):
    return ((x % 2) * 8 + z, ((x // 2) * 4 + y) * 2 + c)


class Links:
    def __init__(self, send_sems, recv_sems):
        self.send_sems = send_sems
        self.recv_sems = recv_sems
        self.used = 0
        self.open = []

    def copy(self, src, dst, peer, index):
        return pltpu.make_async_remote_copy(
            src_ref=src,
            dst_ref=dst,
            send_sem=self.send_sems.at[index],
            recv_sem=self.recv_sems.at[index],
            device_id=peer,
            device_id_type=MESH,
        )

    def send(self, src, dst, peer):
        copy = self.copy(src, dst, peer, self.used)
        self.used += 1
        copy.start()
        self.open.append(copy)
        return copy

    def send_group(self, copies, all_src, all_dst, peer=None):
        index = self.used
        self.used += 1
        for src, dst, to in copies:
            self.copy(src, dst, to, index).start()
        group = self.copy(all_src, all_dst, peer or copies[0][2], index)
        self.open.append(group)
        return group

    def more(self, index, src, dst, peer):
        self.copy(src, dst, peer, index).start()

    def finish(self):
        for copy in self.open:
            copy.wait_send()
        self.open = []


def greet(peers):
    barrier = pltpu.get_barrier_semaphore()
    for peer in peers:
        pl.semaphore_signal(barrier, inc=1, device_id=peer, device_id_type=MESH)
    return lambda: pl.semaphore_wait(barrier, len(peers))


def moe_kernel(
    normed,
    meta_a,
    meta_b,
    hidden,
    w_gate,
    w_up,
    w_down,
    out,
    mix,
    tok,
    stage,
    near,
    far,
    far_stage,
    slot,
    got,
    back,
    acc,
    hid,
    w_in,
    w_out,
    rank_mask,
    rank_mask_t,
    choose,
    scatter,
    part_send,
    part_recv,
    total,
    z_send,
    z_recv,
    far_total,
    far_send,
    far_plus,
    far_minus,
    line_send,
    line_recv,
    core_send,
    core_recv,
    send_sems,
    recv_sems,
    local_sems,
):
    x, y, z, core = place()
    other = 1 - core

    def at(dx=0, dy=0, dz=0, dc=0):
        return device((x + dx) % 4, (y + dy) % 4, (z + dz) % 8, (core + dc) % 2)

    def line(h, d):
        return at(dy=d) if h else at(dx=d)

    def toward(h, d, dc):
        return at(dx=d, dc=dc) if h else at(dy=d, dc=dc)

    sibling = at(dc=1)
    z_up, z_down = at(dz=1), at(dz=7)
    peers = [sibling] + [at(dz=d) for d in range(1, 8)]
    for d in (1, 2, 3):
        for dc in (0, 1):
            peers.append(at(dx=d, dc=dc))
            peers.append(at(dy=d, dc=dc))
    arrived = greet(peers)
    loads = [
        pltpu.make_async_copy(w_gate, w_in.at[:, 0:384], local_sems.at[0]),
        pltpu.make_async_copy(w_up, w_in.at[:, 384:768], local_sems.at[1]),
        pltpu.make_async_copy(w_down, w_out, local_sems.at[2]),
    ]
    for load in loads:
        load.start()

    def columns(k, h, c):
        return pl.ds(pl.multiple_of(k * 2048 + h * 1024 + c * 256, 256), 256)

    own_rows = pl.ds(pl.multiple_of(core * 16, 16), 16)
    for h in (0, 1):
        cols = slice(h * 256, (h + 1) * 256)
        stage[:, cols] = normed[:, columns(other, h, 0)]
        tok[own_rows, cols] = normed[:, columns(core, h, 0)]
        for c in FAR:
            far_stage[c - 1, h] = normed[:, columns(other, h, c)]
            far[c - 1, h, 0, 0, own_rows] = normed[:, columns(core, h, c)]

    links = Links(send_sems, recv_sems)
    arrived()
    swap = links.send(stage, tok.at[own_rows], sibling)
    far_swap = links.send(far_stage, far.at[:, :, 0, 0, own_rows], sibling)
    swap.wait_recv()

    def rows(dz):
        return pl.ds(dz * 32, 32)

    dense = {}

    def spread(dz):
        r = rows(dz)
        dense[dz] = links.send_group(
            [
                (tok.at[r, h * 256 : (h + 1) * 256], near.at[h, 4 - d, r], line(h, d))
                for d in (2, 1, 3)
                for h in (0, 1)
            ],
            near.at[:, 1:4, r],
            near.at[:, 1:4, r],
        )

    ring = {}
    for d in (1, 7, 2, 6, 3, 5, 4):
        ring[8 - d] = links.send(tok.at[rows(0)], tok.at[rows(8 - d)], at(dz=d))
    spread(0)
    far_swap.wait_recv()
    far_line = links.send_group(
        [
            (far.at[:, h, 0, 0], far.at[:, h, 0, 4 - d], line(h, d))
            for d in (2, 1, 3)
            for h in (0, 1)
        ],
        far.at[:, :, 0, 1:4],
        far.at[:, :, 0, 1:4],
    )

    n = lax.broadcasted_iota(jnp.int32, (8, 48, 256), 1)
    t = lax.broadcasted_iota(jnp.int32, (8, 48, 256), 2)
    block = (n * 171) >> 9
    rank_mask[...] = (
        jnp.where(block == (t >> 4), n - 3 * block + 1, -1).astype(F32).reshape(384, 256)
    )
    r = lax.broadcasted_iota(jnp.int32, (256, 384), 1)
    t = lax.broadcasted_iota(jnp.int32, (256, 384), 0)
    n = r - 48 * ((r * 1366) >> 16)
    block = (n * 171) >> 9
    rank_mask_t[...] = jnp.where(block == (t >> 4), n - 3 * block + 1, -1).astype(F32)
    q = lax.broadcasted_iota(jnp.int32, (8, 48, 128), 0)
    lane = lax.broadcasted_iota(jnp.int32, (8, 48, 128), 2)
    step = q >> 1
    to_core = (core + (q & 1)) & 1
    to_y = (y + step) & 3
    to_x = (x + step) & 3
    half = z // 4
    expert_a = 4 * ((x // 2 * 4 + to_y) * 2 + to_core) + 2 * (x % 2) + half
    expert_b = 4 * (((to_x >> 1) * 4 + y) * 2 + to_core) + 2 * (to_x & 1) + half
    metas = (meta_a, meta_b)

    def one_hot(match):
        return jnp.where(match, 1.0, 0.0).astype(BF).reshape(384, 128)

    def masks(h, d):
        expert = expert_b if h else expert_a
        pick = one_hot(lane == expert)
        info = metas[h][d]
        found = lax.dot_general(pick, info, NT, preferred_element_type=F32)
        choose[h, d] = jnp.where(found == rank_mask[...], 1.0, 0.0).astype(BF)
        found = lax.dot_general(info, pick, NT, preferred_element_type=F32)
        scale = lax.dot_general(info, one_hot(lane == expert + 64), NT, preferred_element_type=F32)
        scatter[h, d] = jnp.where(found == rank_mask_t[...], scale, 0.0).astype(BF)

    far_up, far_down = {}, {}

    def far_start(c):
        piece = far.at[c - 1]
        far_up[c] = links.send(piece.at[:, 0], piece.at[:, 7], z_up)
        far_down[c] = links.send(piece.at[:, 0], piece.at[:, 1], z_down)

    def far_step(c, i):
        piece = far.at[c - 1]
        far_up[c].wait_recv()
        far_down[c].wait_recv()
        if i < 3:
            far_up[c] = links.send(piece.at[:, 8 - i], piece.at[:, 7 - i], z_up)
            far_down[c] = links.send(piece.at[:, i], piece.at[:, i + 1], z_down)
        elif i == 3:
            left, right = pl.ds(0, 2), pl.ds(2, 2)
            far_up[c] = links.send(piece.at[:, 5, left], piece.at[:, 4, left], z_up)
            far_down[c] = links.send(piece.at[:, 3, right], piece.at[:, 4, right], z_down)

    for dz in (7, 1):
        ring[dz].wait_recv()
        spread(dz)
    far_line.wait_recv()
    far_start(1)
    masks(0, 0)
    for dz in (6, 2):
        ring[dz].wait_recv()
        spread(dz)
    masks(1, 0)
    for dz in (5, 3):
        ring[dz].wait_recv()
        spread(dz)
    masks(0, 1)
    ring[4].wait_recv()
    spread(4)
    far_start(2)
    masks(1, 1)
    masks(0, 3)
    far_step(1, 1)
    masks(1, 3)
    masks(0, 2)
    masks(1, 2)
    acc[...] = jnp.zeros_like(acc)

    def select(c, h, d):
        if c:
            tokens = far[c - 1, h, :, d].reshape(256, 256)
        elif d == 0:
            tokens = tok[:, h * 256 : (h + 1) * 256]
        else:
            tokens = near[h, d]
        picked = jnp.dot(choose[h, d], tokens, preferred_element_type=F32)
        slot[c, h, SPOS[d]] = picked.astype(BF).reshape(8, 48, 256)

    moved, kept = {}, {}

    def dispatch(c, h):
        for d in (0, 1, 3, 2):
            select(c, h, d)
        copies = []
        for d in (2, 1, 3, 0):
            for dc in (0, 1):
                src = slot.at[c, h, :, d * 2 + dc]
                dst = got.at[c, h, ((4 - d) % 4) * 2 + dc]
                if d == 0 and dc == 0:
                    kept[c, h] = pltpu.make_async_copy(src, dst, local_sems.at[3 + c * 2 + h])
                    kept[c, h].start()
                else:
                    copies.append((src, dst, toward(h, d, dc)))
        moved[c, h] = links.send_group(copies, slot.at[c, h, :, 1:8], got.at[c, h, 1:8])

    def expert_in(c, h):
        kept[c, h].wait()
        moved[c, h].wait_recv()
        for d in (0, 1, 3, 2):
            term = 0
            for dc in (0, 1):
                k = (core + dc) % 2
                term = term + jnp.dot(
                    got[c, h, d * 2 + dc].reshape(192, 256),
                    w_in[columns(k, h, c), :],
                    preferred_element_type=F32,
                )
            if h == 0:
                acc[:, SPOS[d]] += term.reshape(4, 48, 768)
            else:
                acc[SPOS[d]] += term.reshape(4, 48, 768)

    for dz in range(8):
        dense[dz].wait_recv()
    dispatch(0, 0)
    far_step(1, 2)
    dispatch(0, 1)
    far_step(2, 1)
    far_step(1, 3)
    far_start(3)
    for load in loads:
        load.wait()
    far_step(2, 2)
    far_step(1, 4)
    dispatch(1, 0)
    far_step(2, 3)
    far_step(3, 1)
    dispatch(1, 1)
    expert_in(0, 0)
    far_step(2, 4)
    far_step(3, 2)
    dispatch(2, 0)
    dispatch(2, 1)
    far_step(3, 3)
    expert_in(0, 1)
    far_step(3, 4)
    dispatch(3, 0)
    dispatch(3, 1)
    for c in FAR:
        for h in (0, 1):
            expert_in(c, h)
    for i in range(4):
        gate = acc[i, :, :, 0:384]
        hid[i] = (gate / (1.0 + jnp.exp(-gate)) * acc[i, :, :, 384:768]).astype(BF)

    returned = {}

    def expert_out(c, h):
        index = links.used
        returned[c, h] = links.send_group(
            [], got.at[c, h, 1:8], back.at[c, h, :, 1:8], sibling
        )
        for d in (2, 1, 3, 0):
            rows_in = hid[:, SPOS[d]] if h == 0 else hid[SPOS[d]]
            for dc in (0, 1):
                k = (core + dc) % 2
                block_out = (
                    jnp.dot(
                        rows_in.reshape(192, 384),
                        w_out[:, columns(k, h, c)],
                        preferred_element_type=F32,
                    )
                    .astype(BF)
                    .reshape(4, 48, 256)
                )
                if d == 0 and dc == 0:
                    back[c, h, :, 0] = block_out
                    continue
                target = ((4 - d) % 4) * 2 + dc
                got[c, h, d * 2 + dc] = block_out
                links.more(
                    index, got.at[c, h, d * 2 + dc], back.at[c, h, :, target], toward(h, d, dc)
                )

    def combine(c, h, d):
        return jnp.dot(
            scatter[h, d], back[c, h, SPOS[d]].reshape(384, 256), preferred_element_type=F32
        )

    def all_back(c, h):
        returned[c, h].wait_recv()

    def far_open(c):
        for h in (0, 1):
            all_back(c, h)
            for d in range(4):
                far_total[c - 1, h, d] = combine(c, h, d)
        send, left, right = far_send.at[c - 1], pl.ds(0, 2), pl.ds(2, 2)
        send[:, 4] = far_total[c - 1, :, :, 128:160].astype(BF)
        far_up[c] = links.send(send.at[:, 4, left], far_plus.at[c - 1, 3, :, left], z_up)
        far_down[c] = links.send(send.at[:, 4, right], far_minus.at[c - 1, 3, :, right], z_down)

    def far_return(c, i):
        rest = 8 - i
        left, right = slice(0, 2), slice(2, 4)
        send, plus, minus = far_send.at[c - 1], far_plus.at[c - 1], far_minus.at[c - 1]

        def mine(dz, span=slice(0, 4)):
            return far_total[c - 1, :, span, dz * 32 : dz * 32 + 32]

        far_up[c].wait_recv()
        if i == 3:
            send[:, i, left] = (mine(i, left) + plus[i, :, left].astype(F32)).astype(BF)
            send[:, i, right] = mine(i, right).astype(BF)
        else:
            send[:, i] = (mine(i) + plus[i].astype(F32)).astype(BF)
        far_up[c] = links.send(send.at[:, i], plus.at[i - 1], z_up)
        far_down[c].wait_recv()
        if i == 3:
            send[:, rest, left] = mine(rest, left).astype(BF)
            send[:, rest, right] = (mine(rest, right) + minus[i, :, right].astype(F32)).astype(BF)
        else:
            send[:, rest] = (mine(rest) + minus[i].astype(F32)).astype(BF)
        far_down[c] = links.send(send.at[:, rest], minus.at[i - 1], z_down)

    line_moves = {}

    def far_finish(c):
        far_up[c].wait_recv()
        far_down[c].wait_recv()
        ends = (
            far_total[c - 1, :, :, 0:32]
            + far_plus[c - 1, 0].astype(F32)
            + far_minus[c - 1, 0].astype(F32)
        )
        line_send[c - 1] = ends.astype(BF)
        line_moves[c] = links.send_group(
            [
                (line_send.at[c - 1, h, d], line_recv.at[c - 1, h, (4 - d) % 4], line(h, d))
                for d in (2, 1, 3)
                for h in (0, 1)
            ],
            line_send.at[c - 1, :, 1:4],
            line_recv.at[c - 1, :, 1:4],
        )
        far_total[c - 1, :, 0, 0:32] = ends[:, 0]

    def far_join(c):
        line_moves[c].wait_recv()
        for d in (1, 2, 3):
            far_total[c - 1, :, 0, 0:32] += line_recv[c - 1, :, d].astype(F32)

    parts = {}

    def near_part(h):
        all_back(0, h)
        for d in (2, 1, 3):
            part_send[h, d] = combine(0, h, d).astype(BF)
        parts[h] = links.send_group(
            [(part_send.at[h, d], part_recv.at[h, 4 - d], line(h, d)) for d in (2, 1, 3)],
            part_send.at[h, 1:4],
            part_recv.at[h, 1:4],
        )
        total[:, h * 256 : (h + 1) * 256] = combine(0, h, 0)

    def near_join(h):
        parts[h].wait_recv()
        rest = part_recv[h, 1].astype(F32) + part_recv[h, 2].astype(F32)
        total[:, h * 256 : (h + 1) * 256] += rest + part_recv[h, 3].astype(F32)

    def z_return():
        z_send[...] = total[...].reshape(8, 32, 512).astype(BF)
        return links.send_group(
            [(z_send.at[d], z_recv.at[8 - d], at(dz=d)) for d in (4, 3, 5, 2, 6, 1, 7)],
            z_send.at[1:8],
            z_recv.at[1:8],
        )

    for c in (1, 2):
        for h in (0, 1):
            expert_out(c, h)
    far_open(1)
    expert_out(3, 0)
    far_return(1, 3)
    expert_out(3, 1)
    far_return(1, 2)
    far_open(2)
    far_return(1, 1)
    expert_out(0, 0)
    far_return(2, 3)
    expert_out(0, 1)
    far_finish(1)
    far_return(2, 2)
    far_open(3)
    far_return(2, 1)
    far_return(3, 3)
    near_part(0)
    near_part(1)
    far_return(3, 2)
    far_finish(2)
    far_return(3, 1)
    near_join(0)
    near_join(1)
    ending = z_return()
    far_join(1)
    far_join(2)
    far_finish(3)
    far_join(3)
    other_rows = pl.ds(pl.multiple_of(other * 16, 16), 16)
    for h in (0, 1):
        for c in FAR:
            core_send[:, h * 1024 + c * 256 : h * 1024 + (c + 1) * 256] = far_total[
                c - 1, h, 0, other_rows
            ]
            mix[:, columns(core, h, c)] = far_total[c - 1, h, 0, own_rows]
    ending.wait_recv()
    ends = total[0:32]
    for d in range(1, 8):
        ends = ends + z_recv[d].astype(F32)
    total[0:32] = ends
    for h in (0, 1):
        core_send[:, h * 1024 : h * 1024 + 256] = total[other_rows, h * 256 : (h + 1) * 256]
    swap = links.send(core_send, core_recv, sibling)
    for h in (0, 1):
        mix[:, columns(core, h, 0)] = total[own_rows, h * 256 : (h + 1) * 256]
    swap.wait_recv()
    mix[:, pl.ds(pl.multiple_of(other * 2048, 2048), 2048)] = core_recv[...]
    result = hidden[...] + mix[...]
    out[...] = jnp.stack([result[0:8], result[8:16]], axis=1).astype(BF)
    links.finish()


def moe(*operands):
    vmem = pl.BlockSpec(memory_space=pltpu.VMEM)
    hbm = pl.BlockSpec(memory_space=pl.ANY)
    return pl.pallas_call(
        moe_kernel,
        out_shape=jax.ShapeDtypeStruct((8, 2, D), BF),
        in_specs=[vmem, vmem, vmem, vmem, hbm, hbm, hbm],
        out_specs=vmem,
        scratch_shapes=[
            pltpu.VMEM((16, D), F32),
            pltpu.VMEM((256, 512), BF),
            pltpu.VMEM((16, 512), BF),
            pltpu.VMEM((2, 4, 256, 256), BF),
            pltpu.VMEM((3, 2, 8, 4, 32, 256), BF),
            pltpu.VMEM((3, 2, 16, 256), BF),
            pltpu.VMEM((4, 2, 4, 8, 48, 256), BF),
            pltpu.VMEM((4, 2, 8, 4, 48, 256), BF),
            pltpu.VMEM((4, 2, 4, 8, 48, 256), BF),
            pltpu.VMEM((4, 4, 48, 768), F32),
            pltpu.VMEM((4, 4, 48, 384), BF),
            pltpu.VMEM((4096, 768), BF),
            pltpu.VMEM((384, 4096), BF),
            pltpu.VMEM((384, 256), F32),
            pltpu.VMEM((256, 384), F32),
            pltpu.VMEM((2, 4, 384, 256), BF),
            pltpu.VMEM((2, 4, 256, 384), BF),
            pltpu.VMEM((2, 4, 256, 256), BF),
            pltpu.VMEM((2, 4, 256, 256), BF),
            pltpu.VMEM((256, 512), F32),
            pltpu.VMEM((8, 32, 512), BF),
            pltpu.VMEM((8, 32, 512), BF),
            pltpu.VMEM((3, 2, 4, 256, 256), F32),
            pltpu.VMEM((3, 2, 8, 4, 32, 256), BF),
            pltpu.VMEM((3, 4, 2, 4, 32, 256), BF),
            pltpu.VMEM((3, 4, 2, 4, 32, 256), BF),
            pltpu.VMEM((3, 2, 4, 32, 256), BF),
            pltpu.VMEM((3, 2, 4, 32, 256), BF),
            pltpu.VMEM((16, 2048), F32),
            pltpu.VMEM((16, 2048), F32),
            pltpu.SemaphoreType.DMA((MOE_SEMS,)),
            pltpu.SemaphoreType.DMA((MOE_SEMS,)),
            pltpu.SemaphoreType.DMA((16,)),
        ],
        compiler_params=pltpu.CompilerParams(
            collective_id=1, has_side_effects=True, vmem_limit_bytes=60 * 2**20
        ),
        name="moe",
    )(*operands)


ATT_SEMS = 64


def attn_kernel(
    queries,
    keys,
    values,
    prefix_keys,
    prefix_values,
    out_weight,
    residual,
    gain,
    ids_in,
    gates_in,
    hidden,
    normed,
    meta_a,
    meta_b,
    q_raw,
    k_raw,
    v_raw,
    res_raw,
    gain_raw,
    ids,
    gates,
    res,
    kv,
    wts,
    qs,
    pre_k,
    pre_v,
    scores,
    pre_scores,
    top,
    summed,
    weighted,
    att,
    att_bf,
    own_term,
    core_send,
    core_recv,
    y_send,
    y_recv,
    x_keep,
    x_send,
    x_recv,
    info_a,
    info_b,
    send_sems,
    recv_sems,
    local_sems,
):
    x, y, z, core = place()
    other = 1 - core
    x_lo = x % 2
    kv_head = (lax.axis_index("expert")) // 4

    def at(dx=0, dy=0, dz=0, dc=0):
        return device((x + dx) % 4, (y + dy) % 4, (z + dz) % 8, (core + dc) % 2)

    sibling = at(dc=1)
    partner = device(x + 1 - 2 * x_lo, y, z, core)
    z_up, z_down = at(dz=1), at(dz=7)
    peers = [sibling, z_up, z_down, at(dz=2), at(dz=6)]
    for d in (1, 2, 3):
        peers.append(at(dx=d))
        peers.append(at(dy=d))
    arrived = greet(peers)
    head_cols = pl.ds(pl.multiple_of(kv_head * 128, 128), 128)
    loads = [
        pltpu.make_async_copy(src, dst, local_sems.at[i])
        for i, (src, dst) in enumerate(
            (
                (keys.at[:, :, head_cols], k_raw),
                (values.at[:, :, head_cols], v_raw),
                (ids_in, ids),
                (gates_in, gates),
                (out_weight, wts.at[0]),
                (queries, q_raw),
                (prefix_keys.at[:, head_cols], pre_k.at[0:64]),
                (prefix_values.at[:, head_cols], pre_v.at[0:64]),
                (residual, res_raw),
                (gain, gain_raw),
            )
        )
    ]
    for load in loads:
        load.start()
    for load in loads[:4]:
        load.wait()
    for b in range(2):
        kv[core, 0, :, b * 128 : (b + 1) * 128] = jnp.where(
            core == 0, k_raw[:, b, :].astype(F32), v_raw[:, b, :].astype(F32)
        ).astype(BF)
    token_ids = jnp.concatenate([ids[:, 0, :], ids[:, 1, :]], axis=0)
    token_gates = jnp.concatenate([gates[:, 0, :], gates[:, 1, :]], axis=0)
    lane = lax.broadcasted_iota(jnp.int32, (16, 128), 1)
    chosen = jnp.zeros((16, 128), F32)
    weight = jnp.zeros((16, 128), F32)
    for j in range(TOPK):
        column = token_ids[:, j : j + 1]
        chosen = chosen + jnp.where(lane == column, 1.0, 0.0)
        weight = weight + jnp.where(lane == column + 64, token_gates[:, j : j + 1], 0.0)
    row_i = lax.broadcasted_iota(jnp.int32, (16, 16), 0)
    col_i = lax.broadcasted_iota(jnp.int32, (16, 16), 1)
    lower = jnp.where(col_i <= row_i, 1.0, 0.0).astype(BF)
    rank = jnp.dot(lower, chosen.astype(BF), preferred_element_type=F32)
    own_rows = pl.ds(pl.multiple_of(core * 16, 16), 16)
    info_a[0, own_rows] = (rank * chosen + weight).astype(BF)

    links = Links(send_sems, recv_sems)
    arrived()

    def lines(dz):
        return pl.ds(dz * 32, 32)

    info = links.send(info_a.at[0, own_rows], info_a.at[0, own_rows], sibling)
    info_up, info_down = {}, {}

    def info_step(i):
        if i:
            info_up[i].wait_recv()
            info_down[i].wait_recv()
        else:
            info.wait_recv()
        if i < 3:
            src = info_a.at[0, lines((8 - i) % 8)]
            info_up[i + 1] = links.send(src, info_a.at[0, lines(7 - i)], z_up)
            info_down[i + 1] = links.send(
                info_a.at[0, lines(i)], info_a.at[0, lines(i + 1)], z_down
            )
        elif i == 3:
            low, high = pl.ds(4 * 32, 16), pl.ds(4 * 32 + 16, 16)
            info_up[4] = links.send(info_a.at[0, pl.ds(5 * 32, 16)], info_a.at[0, low], z_up)
            info_down[4] = links.send(info_a.at[0, pl.ds(3 * 32 + 16, 16)], info_a.at[0, high], z_down)


    across = {}
    sharing = links.used
    shared = [
        links.send_group([], kv.at[core, pl.ds(i * 8, 8)], kv.at[core, pl.ds(i * 8, 8)], sibling)
        for i in (0, 1)
    ]

    def share(block):
        links.more(sharing + block // 8, kv.at[core, block], kv.at[core, block], sibling)

    def hand_on(dz):
        share(dz)
        across[dz] = links.send(kv.at[core, dz], kv.at[core, 8 + dz], partner)

    def hand_over(dz):
        across[dz].wait_recv()
        share(8 + dz)

    w_up, w_down = {}, {}

    def w_start(s):
        r = pl.ds(s * 256, 256)
        w_up[s] = links.send(wts.at[0, r], wts.at[7, r], z_up)
        w_down[s] = links.send(wts.at[0, r], wts.at[1, r], z_down)

    def w_step(s, i):
        r = pl.ds(s * 256, 256)
        w_up[s].wait_recv()
        w_down[s].wait_recv()
        if i < 3:
            w_up[s] = links.send(wts.at[8 - i, r], wts.at[7 - i, r], z_up)
            w_down[s] = links.send(wts.at[i, r], wts.at[i + 1, r], z_down)
        elif i == 3:
            first, second = pl.ds(s * 256, 128), pl.ds(s * 256 + 128, 128)
            w_up[s] = links.send(wts.at[5, first], wts.at[4, first], z_up)
            w_down[s] = links.send(wts.at[3, second], wts.at[4, second], z_down)

    low, high = pl.ds(0, 64), pl.ds(64, 64)
    ring = {}
    for d in (1, 7, 2, 6):
        ring[8 - d] = links.send(kv.at[core, 0], kv.at[core, 8 - d], at(dz=d))
    hand_on(0)
    info_step(0)

    for load in loads[4:]:
        load.wait()
    for b in range(2):
        for h in range(4):
            qs[b, h * 128 : (h + 1) * 128, :] = q_raw[:, b, h * 128 : (h + 1) * 128]
    pre_k[64:128] = jnp.zeros((64, 128), BF)
    pre_v[64:128] = jnp.zeros((64, 128), BF)

    for dz in (7, 1):
        ring[dz].wait_recv()
        hand_on(dz)
    w_start(0)
    w_start(1)
    for dz, part, peer, far in ((6, low, z_up, at(dz=2)), (2, high, z_down, at(dz=6))):
        ring[dz].wait_recv()
        ring[5 if dz == 6 else 3] = links.send(
            kv.at[core, dz], kv.at[core, 5 if dz == 6 else 3], peer
        )
        ring[4, dz] = links.send(kv.at[core, dz, part], kv.at[core, 4, part], far)
        hand_on(dz)
    hand_over(0)
    info_step(1)
    hand_over(7)
    hand_over(1)
    info_step(2)
    for dz in (5, 3):
        ring[dz].wait_recv()
        hand_on(dz)
    ring[4, 6].wait_recv()
    ring[4, 2].wait_recv()
    hand_on(4)
    w_step(0, 1)
    hand_over(6)
    hand_over(2)
    w_step(1, 1)
    info_step(3)
    hand_over(5)
    hand_over(3)
    hand_over(4)
    info_step(4)
    info_moves = [
        links.send_group(
            [(info_a.at[0], dst.at[4 - d], at(**{axis: d})) for d in (1, 2, 3)],
            dst.at[1:4],
            dst.at[1:4],
        )
        for dst, axis in ((info_a, "dx"), (info_b, "dy"))
    ]
    for b in range(2):
        res[b * 8 : (b + 1) * 8] = res_raw[:, b, :].astype(F32)

    scale = 1.0 / math.sqrt(HD)
    gap = lax.broadcasted_iota(jnp.int32, (4, 128, 128), 2) - lax.broadcasted_iota(
        jnp.int32, (4, 128, 128), 1
    )
    gap = gap.reshape(512, 128)
    pre_lane = lax.broadcasted_iota(jnp.int32, (512, 128), 1)

    def attend_start(b):
        first = lax.dot_general(qs[b], pre_k[...], NT, preferred_element_type=F32) * scale
        first = jnp.where(pre_lane < 64, first, -1e30)
        pre_scores[b] = first
        top[b] = first

    def attend_scores(b, half):
        cols = slice(b * 128, (b + 1) * 128)

        def score(c, carry):
            block = lax.dot_general(
                qs[b],
                kv[0, pl.ds(2 * c, 2), :, cols].reshape(256, 128),
                NT,
                preferred_element_type=F32,
            )
            best = top[b]
            for r in range(2):
                theirs = ((x_lo + c // 4) % 2) * 8 + (z + 2 * c + r) % 8
                ahead = (x_lo * 8 + z - theirs) * 128
                part = jnp.where(gap <= ahead, block[:, r * 128 : (r + 1) * 128] * scale, -1e30)
                scores[b, c, :, r * 128 : (r + 1) * 128] = part
                best = jnp.maximum(best, part)
            top[b] = best
            return carry

        lax.fori_loop(half * 4, half * 4 + 4, score, 0)

    def attend_mix(b):
        cols = slice(b * 128, (b + 1) * 128)
        top[b] = jnp.broadcast_to(jnp.max(top[b], -1, keepdims=True), (512, 128))
        probs = jnp.exp(pre_scores[b] - top[b]).astype(BF)
        summed[...] = probs.astype(F32)
        weighted[...] = jnp.dot(probs, pre_v[...], preferred_element_type=F32)

        def mix(c, carry):
            peak = top[b]
            left = jnp.exp(scores[b, c, :, 0:128] - peak).astype(BF)
            right = jnp.exp(scores[b, c, :, 128:256] - peak).astype(BF)
            summed[...] += left.astype(F32) + right.astype(F32)
            weighted[...] += jnp.dot(
                jnp.concatenate([left, right], axis=1),
                kv[1, pl.ds(2 * c, 2), :, cols].reshape(256, 128),
                preferred_element_type=F32,
            )
            return carry

        lax.fori_loop(0, 8, mix, 0)
        result = weighted[...] / jnp.sum(summed[...], -1, keepdims=True)
        for h in range(4):
            for e in range(16):
                start = h * 128 + e * 8
                att[b, e % 2, (e // 2) % 4, e // 8, :, h * 128 : (h + 1) * 128] = result[
                    start : start + 8
                ]

        att_bf[0, b] = att[b].reshape(128, 512).astype(BF)
        return links.send(att_bf.at[0, b], att_bf.at[1, b], partner)

    attend_start(0)
    attend_start(1)
    shared[0].wait_recv()
    attend_scores(0, 0)
    attend_scores(1, 0)
    w_step(0, 2)
    w_step(1, 2)
    shared[1].wait_recv()
    attend_scores(0, 1)
    attend_scores(1, 1)
    w_step(0, 3)
    swaps = [attend_mix(0)]
    w_step(1, 3)
    swaps.append(attend_mix(1))
    for copy in info_moves:
        copy.wait_recv()
    meta_a[...] = info_a[...]
    meta_b[0] = info_a[0]
    meta_b[1:4] = info_b[1:4]
    for swap in swaps:
        swap.wait_recv()

    def half(c):
        rows = pl.ds(pl.multiple_of(c * 64, 64), 64)
        return att_bf[:, :, rows, :].reshape(256, 512)

    chunks = ((0, 7), (1, 6), (2, 5), (3, 4))
    core_moves, y_moves, x_moves = {}, {}, {}

    def project(j):
        if j == 3:
            w_step(0, 4)
            w_step(1, 4)
        for i, dz in enumerate(chunks[j]):
            cols = slice(i * 256, (i + 1) * 256)
            core_send[j, :, :, :, :, cols] = (
                jnp.dot(half(other), wts[dz], preferred_element_type=F32)
                .astype(BF)
                .reshape(2, 2, 4, 16, 256)
            )
        core_moves[j] = links.send(core_send.at[j], core_recv.at[j], sibling)
        for i, dz in enumerate(chunks[j]):
            cols = slice(i * 256, (i + 1) * 256)
            own_term[j, :, :, :, :, cols] = jnp.dot(
                half(core), wts[dz], preferred_element_type=F32
            ).reshape(2, 2, 4, 16, 256)

    def along_y(j):
        core_moves[j].wait_recv()
        both = own_term[j] + core_recv[j].astype(F32)
        own_term[j] = both
        y_send[j] = both.astype(BF)
        y_moves[j] = links.send_group(
            [
                (y_send.at[j, :, :, (y + d) % 4], y_recv.at[j, 4 - d], at(dy=d))
                for d in (2, 1, 3)
            ],
            y_recv.at[j, 1:4],
            y_recv.at[j, 1:4],
        )

    def along_x(j):
        own = own_term[j, :, :, y]
        y_moves[j].wait_recv()
        for d in (1, 2, 3):
            own = own + y_recv[j, d].astype(F32)
        for p in range(2):
            for i in range(2):
                tile = jnp.concatenate(
                    [own[p, 0, i * 8 : i * 8 + 8], own[p, 1, i * 8 : i * 8 + 8]], axis=0
                )
                x_keep[j, p, i] = tile
                x_send[j, p, i] = tile.astype(BF)
        x_moves[j] = links.send_group(
            [
                (x_send.at[j, d % 2, ((x + d) % 4) // 2], x_recv.at[j, 4 - d], at(dx=d))
                for d in (2, 1, 3)
            ],
            x_recv.at[j, 1:4],
            x_recv.at[j, 1:4],
        )

    square = jnp.zeros((16, 128), F32)

    def join(j, square):
        x_moves[j].wait_recv()
        mine = x_keep[j, 0, x // 2] + x_recv[j, 2].astype(F32)
        theirs = x_recv[j, 1].astype(F32) + x_recv[j, 3].astype(F32)
        for i, dz in enumerate(chunks[j]):
            for side, part in ((x_lo, mine), (1 - x_lo, theirs)):
                where = pl.ds(pl.multiple_of((side * 8 + (z + dz) % 8) * 256, 256), 256)
                value = res[:, where] + part[:, i * 256 : (i + 1) * 256]
                hidden[:, where] = value
                value = value * value
                square = square + value[:, 0:128] + value[:, 128:256]
        return square

    project(0)
    project(1)
    along_y(0)
    project(2)
    along_y(1)
    project(3)
    along_y(2)
    along_x(0)
    along_y(3)
    for j in (1, 2, 3):
        along_x(j)
    for j in range(4):
        square = join(j, square)
    mean = jnp.sum(square, -1, keepdims=True) * (1.0 / D)
    normed[...] = (hidden[...] * lax.rsqrt(mean + 1e-06) * gain_raw[...].reshape(1, D).astype(F32)).astype(BF)
    links.finish()


def attention(*operands):
    vmem = pl.BlockSpec(memory_space=pltpu.VMEM)
    hbm = pl.BlockSpec(memory_space=pl.ANY)
    return pl.pallas_call(
        attn_kernel,
        out_shape=(
            jax.ShapeDtypeStruct((16, D), F32),
            jax.ShapeDtypeStruct((16, D), BF),
            jax.ShapeDtypeStruct((4, 256, 128), BF),
            jax.ShapeDtypeStruct((4, 256, 128), BF),
        ),
        in_specs=[hbm] * 10,
        out_specs=(vmem,) * 4,
        scratch_shapes=[
            pltpu.VMEM((128, 2, 512), BF),
            pltpu.VMEM((128, 2, 128), BF),
            pltpu.VMEM((128, 2, 128), BF),
            pltpu.VMEM((8, 2, D), BF),
            pltpu.VMEM((D,), BF),
            pltpu.VMEM((8, 2, TOPK), jnp.int32),
            pltpu.VMEM((8, 2, TOPK), F32),
            pltpu.VMEM((16, D), F32),
            pltpu.VMEM((2, 16, 128, 256), BF),
            pltpu.VMEM((8, 512, 256), BF),
            pltpu.VMEM((2, 512, 128), BF),
            pltpu.VMEM((128, 128), BF),
            pltpu.VMEM((128, 128), BF),
            pltpu.VMEM((2, 8, 512, 256), F32),
            pltpu.VMEM((2, 512, 128), F32),
            pltpu.VMEM((2, 512, 128), F32),
            pltpu.VMEM((512, 128), F32),
            pltpu.VMEM((512, 128), F32),
            pltpu.VMEM((2, 2, 4, 2, 8, 512), F32),
            pltpu.VMEM((2, 2, 128, 512), BF),
            pltpu.VMEM((4, 2, 2, 4, 16, 512), F32),
            pltpu.VMEM((4, 2, 2, 4, 16, 512), BF),
            pltpu.VMEM((4, 2, 2, 4, 16, 512), BF),
            pltpu.VMEM((4, 2, 2, 4, 16, 512), BF),
            pltpu.VMEM((4, 4, 2, 2, 16, 512), BF),
            pltpu.VMEM((4, 2, 2, 16, 512), F32),
            pltpu.VMEM((4, 2, 2, 16, 512), BF),
            pltpu.VMEM((4, 4, 16, 512), BF),
            pltpu.VMEM((4, 256, 128), BF),
            pltpu.VMEM((4, 256, 128), BF),
            pltpu.SemaphoreType.DMA((ATT_SEMS,)),
            pltpu.SemaphoreType.DMA((ATT_SEMS,)),
            pltpu.SemaphoreType.DMA((10,)),
        ],
        compiler_params=pltpu.CompilerParams(
            collective_id=2, has_side_effects=True, vmem_limit_bytes=60 * 2**20
        ),
        name="attention",
    )(*operands)


def shards(
    queries,
    keys,
    values,
    prefix_keys,
    prefix_values,
    out_weight,
    residual_in,
    norm_gain,
    expert_ids,
    route_weights,
    w_gate,
    w_up,
    w_down,
):
    hidden_state, normed, meta_a, meta_b = attention(
        queries,
        keys,
        values,
        prefix_keys,
        prefix_values,
        out_weight,
        residual_in,
        norm_gain,
        expert_ids,
        route_weights,
    )
    return moe(
        normed, meta_a, meta_b, hidden_state, w_gate[0, 0], w_up[0, 0], w_down[0, 0]
    )


def solution(mesh):
    in_specs = (
        P("seq", None, "expert"),
        P("seq", None, None),
        P("seq", None, None),
        P(),
        P(),
        P("expert", "seq"),
        P(("seq", "expert"), None, None),
        P(),
        P(("seq", "expert"), None, None),
        P(("seq", "expert"), None, None),
        P("seq", "expert", None, None),
        P("seq", "expert", None, None),
        P("seq", "expert", None, None),
    )
    out_specs = P(("seq", "expert"), None, None)
    return jax.shard_map(shards, mesh=mesh, in_specs=in_specs, out_specs=out_specs, check_vma=False)
```

time: 230 us -> 202 us (0.88)
  Pallas kernels: 218 us -> 200 us
  local copies, waits for them, and re-layouts: 9.93 us -> 1.65 us
    pallas_call x1, Pallas kernels: 152 us -> 132 us  [moe(): pl.pallas_call(moe_kernel, out_shape=jax.ShapeDtypeStruct((8, 2, D), BF),...]
    unnamed x15 -> x1, local copies, waits for them, and re-layouts: 6.25 us -> 1.65 us
    reshape x4 -> x0, local copies, waits for them, and re-layouts: 2.7 us -> none  [the longest x2 1.19 us: by_sequence(): return jnp.transpose(array, (1, 0, 2)).reshape(16, array.shape[-1])]
where the time goes in v3:
time: 202 us
  Pallas kernels  200 us (99%)
    pallas_call x1, Pallas kernels, moe(): pl.pallas_call(moe_kernel, out_shape=jax.ShapeDtypeStruct((8, 2, D), BF),...  132 us
    pallas_call x1, Pallas kernels, attention(): pl.pallas_call(attn_kernel, out_shape=(jax.ShapeDtypeStruct((16, D), F32)...  67.6 us

profile of v3, /device:TPU:1, one launch (start us, length us, event | category | flops | bytes accessed | tf_op | source)
XLA Modules:
  0.0 201.6 jit_solution(4359275488858814364)
XLA Ops:
  0.0 67.6 %attention.1 = (f32[16,4096]{1,0:T(8,128)}, bf16[16,4096]{1,0:T(8,128)(2,1)}, bf16[4,256,128]{2,1,0:T(8,128)(2,1)}, bf16[4,256,128]{2,1,0:T(8,128)(2,1)}) custom-call(bf16[128,2,512]{2,1,0:T(2,128)(2,1)} %queries.1, bf16[128,2,512]{2,1,0:T(2,128)(2,1)} %keys.1, bf16[128,2,512]{2,1,0:T(2,128)(2,1)} %values.1, bf16[64,512]{1,0:T(8,128)(2,1)} %prefix_keys.1, ...), custom_call_target="tpu_custom_call" | custom-call | tf_op jit(solution)/shard_map/attention/pallas_call | solution.py:1003
  67.6 132.3 %moe.1 = bf16[8,2,4096]{2,1,0:T(2,128)(2,1)} custom-call(bf16[16,4096]{1,0:T(8,128)(2,1)} %get-tuple-element.9.normed, bf16[4,256,128]{2,1,0:T(8,128)(2,1)} %get-tuple-element.10.meta_a, bf16[4,256,128]{2,1,0:T(8,128)(2,1)} %get-tuple-element.11.meta_b, f32[16,4096]{1,0:T(8,128)} %get-tuple-element.12.hidden, bf16[4096,384]{1,0:T(8,128)(2,1)} %bitcast.3, ...), custom_call_target="tpu_custom_call" | custom-call | tf_op jit(solution)/shard_map/moe/pallas_call | solution.py:540
  200.0 1.7 copy.15

commit v4 on v3

--- a/solution.py
+++ b/solution.py
@@ -137,7 +137,7 @@
 
     sibling = at(dc=1)
     z_up, z_down = at(dz=1), at(dz=7)
-    peers = [sibling] + [at(dz=d) for d in range(1, 8)]
+    peers = [sibling] + [at(dz=d, dc=dc) for d in range(1, 8) for dc in (0, 1)]
     for d in (1, 2, 3):
         for dc in (0, 1):
             peers.append(at(dx=d, dc=dc))
@@ -165,7 +165,21 @@
 
     links = Links(send_sems, recv_sems)
     arrived()
+    def own_at(dz):
+        return pl.ds(pl.multiple_of(dz * 32 + core * 16, 16), 16)
+
     swap = links.send(stage, tok.at[own_rows], sibling)
+    ring = {}
+    for d in (1, 7, 2, 6, 3, 5, 4):
+        whole = tok.at[pl.ds((8 - d) * 32, 32)]
+        ring[8 - d] = links.send_group(
+            [
+                (src, tok.at[own_at(8 - d)], at(dz=d, dc=dc))
+                for dc, src in ((0, tok.at[own_rows]), (1, stage))
+            ],
+            whole,
+            whole,
+        )
     far_swap = links.send(far_stage, far.at[:, :, 0, 0, own_rows], sibling)
     swap.wait_recv()
 
@@ -186,9 +200,6 @@
             near.at[:, 1:4, r],
         )
 
-    ring = {}
-    for d in (1, 7, 2, 6, 3, 5, 4):
-        ring[8 - d] = links.send(tok.at[rows(0)], tok.at[rows(8 - d)], at(dz=d))
     spread(0)
     far_swap.wait_recv()
     far_line = links.send_group(
@@ -255,23 +266,18 @@
             far_up[c] = links.send(piece.at[:, 5, left], piece.at[:, 4, left], z_up)
             far_down[c] = links.send(piece.at[:, 3, right], piece.at[:, 4, right], z_down)
 
+    masks(0, 0)
+    masks(1, 0)
     for dz in (7, 1):
         ring[dz].wait_recv()
         spread(dz)
     far_line.wait_recv()
     far_start(1)
-    masks(0, 0)
-    for dz in (6, 2):
+    for dz in (6, 2, 5, 3, 4):
         ring[dz].wait_recv()
         spread(dz)
-    masks(1, 0)
-    for dz in (5, 3):
-        ring[dz].wait_recv()
-        spread(dz)
+    far_start(2)
     masks(0, 1)
-    ring[4].wait_recv()
-    spread(4)
-    far_start(2)
     masks(1, 1)
     masks(0, 3)
     far_step(1, 1)
@@ -458,13 +464,11 @@
 
     def near_part(h):
         all_back(0, h)
+        index = links.used
+        parts[h] = links.send_group([], part_send.at[h, 1:4], part_recv.at[h, 1:4], line(h, 1))
         for d in (2, 1, 3):
             part_send[h, d] = combine(0, h, d).astype(BF)
-        parts[h] = links.send_group(
-            [(part_send.at[h, d], part_recv.at[h, 4 - d], line(h, d)) for d in (2, 1, 3)],
-            part_send.at[h, 1:4],
-            part_recv.at[h, 1:4],
-        )
+            links.more(index, part_send.at[h, d], part_recv.at[h, 4 - d], line(h, d))
         total[:, h * 256 : (h + 1) * 256] = combine(0, h, 0)
 
     def near_join(h):
@@ -473,12 +477,17 @@
         total[:, h * 256 : (h + 1) * 256] += rest + part_recv[h, 3].astype(F32)
 
     def z_return():
-        z_send[...] = total[...].reshape(8, 32, 512).astype(BF)
-        return links.send_group(
-            [(z_send.at[d], z_recv.at[8 - d], at(dz=d)) for d in (4, 3, 5, 2, 6, 1, 7)],
+        z_send[...] = total[...].reshape(8, 2, 16, 512).astype(BF)
+        far_side = links.send_group(
+            [
+                (z_send.at[d, (core + dc) % 2], z_recv.at[8 - d, dc], at(dz=d, dc=dc))
+                for d in (4, 3, 5, 2, 6, 1, 7)
+                for dc in (0, 1)
+            ],
             z_send.at[1:8],
             z_recv.at[1:8],
         )
+        return far_side, links.send(z_send.at[0, other], z_recv.at[0, 1], sibling)
 
     for c in (1, 2):
         for h in (0, 1):
@@ -513,24 +522,28 @@
     other_rows = pl.ds(pl.multiple_of(other * 16, 16), 16)
     for h in (0, 1):
         for c in FAR:
-            core_send[:, h * 1024 + c * 256 : h * 1024 + (c + 1) * 256] = far_total[
-                c - 1, h, 0, other_rows
-            ]
-            mix[:, columns(core, h, c)] = far_total[c - 1, h, 0, own_rows]
-    ending.wait_recv()
-    ends = total[0:32]
-    for d in range(1, 8):
-        ends = ends + z_recv[d].astype(F32)
-    total[0:32] = ends
-    for h in (0, 1):
-        core_send[:, h * 1024 : h * 1024 + 256] = total[other_rows, h * 256 : (h + 1) * 256]
+            core_send[h * 3 + c - 1] = far_total[c - 1, h, 0, other_rows].astype(BF)
     swap = links.send(core_send, core_recv, sibling)
     for h in (0, 1):
-        mix[:, columns(core, h, 0)] = total[own_rows, h * 256 : (h + 1) * 256]
+        for c in FAR:
+            mix[:, columns(core, h, c)] = far_total[c - 1, h, 0, own_rows]
     swap.wait_recv()
-    mix[:, pl.ds(pl.multiple_of(other * 2048, 2048), 2048)] = core_recv[...]
+    for h in (0, 1):
+        for c in FAR:
+            mix[:, columns(other, h, c)] = core_recv[h * 3 + c - 1].astype(F32)
+    for copy in ending:
+        copy.wait_recv()
+    ends = total[own_rows]
+    beside = z_recv[0, 1].astype(F32)
+    for d in range(1, 8):
+        ends = ends + z_recv[d, 0].astype(F32)
+        beside = beside + z_recv[d, 1].astype(F32)
+    for h in (0, 1):
+        mix[:, columns(core, h, 0)] = ends[:, h * 256 : (h + 1) * 256]
+        mix[:, columns(other, h, 0)] = beside[:, h * 256 : (h + 1) * 256]
     result = hidden[...] + mix[...]
     out[...] = jnp.stack([result[0:8], result[8:16]], axis=1).astype(BF)
+    assert links.used <= MOE_SEMS
     links.finish()
 
 
@@ -563,16 +576,16 @@
             pltpu.VMEM((2, 4, 256, 256), BF),
             pltpu.VMEM((2, 4, 256, 256), BF),
             pltpu.VMEM((256, 512), F32),
-            pltpu.VMEM((8, 32, 512), BF),
-            pltpu.VMEM((8, 32, 512), BF),
+            pltpu.VMEM((8, 2, 16, 512), BF),
+            pltpu.VMEM((8, 2, 16, 512), BF),
             pltpu.VMEM((3, 2, 4, 256, 256), F32),
             pltpu.VMEM((3, 2, 8, 4, 32, 256), BF),
             pltpu.VMEM((3, 4, 2, 4, 32, 256), BF),
             pltpu.VMEM((3, 4, 2, 4, 32, 256), BF),
             pltpu.VMEM((3, 2, 4, 32, 256), BF),
             pltpu.VMEM((3, 2, 4, 32, 256), BF),
-            pltpu.VMEM((16, 2048), F32),
-            pltpu.VMEM((16, 2048), F32),
+            pltpu.VMEM((6, 16, 256), BF),
+            pltpu.VMEM((6, 16, 256), BF),
             pltpu.SemaphoreType.DMA((MOE_SEMS,)),
             pltpu.SemaphoreType.DMA((MOE_SEMS,)),
             pltpu.SemaphoreType.DMA((16,)),
@@ -584,7 +597,7 @@
     )(*operands)
 
 
-ATT_SEMS = 64
+ATT_SEMS = 80
 
 
 def attn_kernel(
@@ -646,6 +659,9 @@
 
     sibling = at(dc=1)
     partner = device(x + 1 - 2 * x_lo, y, z, core)
+    y_partner = device(x, y + 1 - 2 * (y % 2), z, core)
+    mine = pl.ds(pl.multiple_of((y % 2) * 64, 64), 64)
+    theirs = pl.ds(pl.multiple_of((1 - y % 2) * 64, 64), 64)
     z_up, z_down = at(dz=1), at(dz=7)
     peers = [sibling, z_up, z_down, at(dz=2), at(dz=6)]
     for d in (1, 2, 3):
@@ -721,23 +737,30 @@
             info_down[4] = links.send(info_a.at[0, pl.ds(3 * 32 + 16, 16)], info_a.at[0, high], z_down)
 
 
-    across = {}
+    across, beside = {}, {}
     sharing = links.used
     shared = [
         links.send_group([], kv.at[core, pl.ds(i * 8, 8)], kv.at[core, pl.ds(i * 8, 8)], sibling)
         for i in (0, 1)
     ]
 
-    def share(block):
-        links.more(sharing + block // 8, kv.at[core, block], kv.at[core, block], sibling)
+    def share(block, rows=pl.ds(0, 128)):
+        piece = kv.at[core, block, rows]
+        links.more(sharing + block // 8, piece, piece, sibling)
 
     def hand_on(dz):
         share(dz)
-        across[dz] = links.send(kv.at[core, dz], kv.at[core, 8 + dz], partner)
+        across[dz] = links.send(kv.at[core, dz, mine], kv.at[core, 8 + dz, mine], partner)
 
     def hand_over(dz):
         across[dz].wait_recv()
-        share(8 + dz)
+        piece = kv.at[core, 8 + dz, mine]
+        beside[dz] = links.send(piece, piece, y_partner)
+        share(8 + dz, mine)
+
+    def hand_last(dz):
+        beside[dz].wait_recv()
+        share(8 + dz, theirs)
 
     w_up, w_down = {}, {}
 
@@ -789,6 +812,7 @@
     info_step(1)
     hand_over(7)
     hand_over(1)
+    hand_last(0)
     info_step(2)
     for dz in (5, 3):
         ring[dz].wait_recv()
@@ -796,15 +820,21 @@
     ring[4, 6].wait_recv()
     ring[4, 2].wait_recv()
     hand_on(4)
-    w_step(0, 1)
     hand_over(6)
     hand_over(2)
-    w_step(1, 1)
+    hand_last(7)
+    hand_last(1)
+    w_step(0, 1)
     info_step(3)
     hand_over(5)
     hand_over(3)
+    hand_last(6)
+    hand_last(2)
+    w_step(1, 1)
     hand_over(4)
     info_step(4)
+    hand_last(5)
+    hand_last(3)
     info_moves = [
         links.send_group(
             [(info_a.at[0], dst.at[4 - d], at(**{axis: d})) for d in (1, 2, 3)],
@@ -841,8 +871,8 @@
             )
             best = top[b]
             for r in range(2):
-                theirs = ((x_lo + c // 4) % 2) * 8 + (z + 2 * c + r) % 8
-                ahead = (x_lo * 8 + z - theirs) * 128
+                source = ((x_lo + c // 4) % 2) * 8 + (z + 2 * c + r) % 8
+                ahead = (x_lo * 8 + z - source) * 128
                 part = jnp.where(gap <= ahead, block[:, r * 128 : (r + 1) * 128] * scale, -1e30)
                 scores[b, c, :, r * 128 : (r + 1) * 128] = part
                 best = jnp.maximum(best, part)
@@ -886,6 +916,7 @@
     attend_start(1)
     shared[0].wait_recv()
     attend_scores(0, 0)
+    hand_last(4)
     attend_scores(1, 0)
     w_step(0, 2)
     w_step(1, 2)
@@ -896,56 +927,46 @@
     swaps = [attend_mix(0)]
     w_step(1, 3)
     swaps.append(attend_mix(1))
-    for copy in info_moves:
-        copy.wait_recv()
-    meta_a[...] = info_a[...]
-    meta_b[0] = info_a[0]
-    meta_b[1:4] = info_b[1:4]
-    for swap in swaps:
-        swap.wait_recv()
-
-    def half(c):
+    def half(p, c):
         rows = pl.ds(pl.multiple_of(c * 64, 64), 64)
-        return att_bf[:, :, rows, :].reshape(256, 512)
+        return att_bf[p, :, rows, :].reshape(128, 512)
 
     chunks = ((0, 7), (1, 6), (2, 5), (3, 4))
     core_moves, y_moves, x_moves = {}, {}, {}
 
-    def project(j):
-        if j == 3:
-            w_step(0, 4)
-            w_step(1, 4)
+    def project(j, p):
         for i, dz in enumerate(chunks[j]):
             cols = slice(i * 256, (i + 1) * 256)
-            core_send[j, :, :, :, :, cols] = (
-                jnp.dot(half(other), wts[dz], preferred_element_type=F32)
+            core_send[j, p, :, :, :, cols] = (
+                jnp.dot(half(p, other), wts[dz], preferred_element_type=F32)
                 .astype(BF)
-                .reshape(2, 2, 4, 16, 256)
+                .reshape(2, 4, 16, 256)
             )
-        core_moves[j] = links.send(core_send.at[j], core_recv.at[j], sibling)
+        core_moves[j, p] = links.send(core_send.at[j, p], core_recv.at[j, p], sibling)
         for i, dz in enumerate(chunks[j]):
             cols = slice(i * 256, (i + 1) * 256)
-            own_term[j, :, :, :, :, cols] = jnp.dot(
-                half(core), wts[dz], preferred_element_type=F32
-            ).reshape(2, 2, 4, 16, 256)
-
-    def along_y(j):
-        core_moves[j].wait_recv()
-        both = own_term[j] + core_recv[j].astype(F32)
-        own_term[j] = both
-        y_send[j] = both.astype(BF)
-        y_moves[j] = links.send_group(
+            own_term[j, p, :, :, :, cols] = jnp.dot(
+                half(p, core), wts[dz], preferred_element_type=F32
+            ).reshape(2, 4, 16, 256)
+
+    def along_y(j, p):
+        core_moves[j, p].wait_recv()
+        both = own_term[j, p] + core_recv[j, p].astype(F32)
+        own_term[j, p] = both
+        y_send[j, p] = both.astype(BF)
+        y_moves[j, p] = links.send_group(
             [
-                (y_send.at[j, :, :, (y + d) % 4], y_recv.at[j, 4 - d], at(dy=d))
+                (y_send.at[j, p, :, (y + d) % 4], y_recv.at[j, 4 - d, p], at(dy=d))
                 for d in (2, 1, 3)
             ],
-            y_recv.at[j, 1:4],
-            y_recv.at[j, 1:4],
+            y_recv.at[j, 1:4, p],
+            y_recv.at[j, 1:4, p],
         )
 
     def along_x(j):
         own = own_term[j, :, :, y]
-        y_moves[j].wait_recv()
+        y_moves[j, 0].wait_recv()
+        y_moves[j, 1].wait_recv()
         for d in (1, 2, 3):
             own = own + y_recv[j, d].astype(F32)
         for p in range(2):
@@ -979,21 +1000,40 @@
                 square = square + value[:, 0:128] + value[:, 128:256]
         return square
 
-    project(0)
-    project(1)
-    along_y(0)
-    project(2)
-    along_y(1)
-    project(3)
-    along_y(2)
+    project(0, 0)
+    project(1, 0)
+    along_y(0, 0)
+    project(2, 0)
+    along_y(1, 0)
+    w_step(0, 4)
+    w_step(1, 4)
+    project(3, 0)
+    along_y(2, 0)
+    for copy in info_moves:
+        copy.wait_recv()
+    meta_a[...] = info_a[...]
+    meta_b[0] = info_a[0]
+    meta_b[1:4] = info_b[1:4]
+    for swap in swaps:
+        swap.wait_recv()
+
+    project(0, 1)
+    along_y(3, 0)
+    project(1, 1)
+    along_y(0, 1)
+    project(2, 1)
+    along_y(1, 1)
+    project(3, 1)
+    along_y(2, 1)
     along_x(0)
-    along_y(3)
+    along_y(3, 1)
     for j in (1, 2, 3):
         along_x(j)
     for j in range(4):
         square = join(j, square)
     mean = jnp.sum(square, -1, keepdims=True) * (1.0 / D)
     normed[...] = (hidden[...] * lax.rsqrt(mean + 1e-06) * gain_raw[...].reshape(1, D).astype(F32)).astype(BF)
+    assert links.used <= ATT_SEMS
     links.finish()
 
 

time: 202 us -> 196 us (0.970)
  Pallas kernels: 200 us -> 194 us
    pallas_call x1, Pallas kernels: 67.6 us -> 63.5 us  [attention(): pl.pallas_call(attn_kernel, out_shape=(jax.ShapeDtypeStruct((16, D), F32)...]
where the time goes in v4:
time: 196 us
  Pallas kernels  194 us (99%)
    pallas_call x1, Pallas kernels, moe(): pl.pallas_call(moe_kernel, out_shape=jax.ShapeDtypeStruct((8, 2, D), BF),...  131 us
    pallas_call x1, Pallas kernels, attention(): pl.pallas_call(attn_kernel, out_shape=(jax.ShapeDtypeStruct((16, D), F32)...  63.5 us

profile of v4, /device:TPU:1, one launch (start us, length us, event | category | flops | bytes accessed | tf_op | source)
XLA Modules:
  0.0 195.7 jit_solution(2735975264796849619)
XLA Ops:
  0.0 63.5 %attention.1 = (f32[16,4096]{1,0:T(8,128)}, bf16[16,4096]{1,0:T(8,128)(2,1)}, bf16[4,256,128]{2,1,0:T(8,128)(2,1)}, bf16[4,256,128]{2,1,0:T(8,128)(2,1)}) custom-call(bf16[128,2,512]{2,1,0:T(2,128)(2,1)} %queries.1, bf16[128,2,512]{2,1,0:T(2,128)(2,1)} %keys.1, bf16[128,2,512]{2,1,0:T(2,128)(2,1)} %values.1, bf16[64,512]{1,0:T(8,128)(2,1)} %prefix_keys.1, ...), custom_call_target="tpu_custom_call" | custom-call | tf_op jit(solution)/shard_map/attention/pallas_call | solution.py:1043
  63.5 130.5 %moe.1 = bf16[8,2,4096]{2,1,0:T(2,128)(2,1)} custom-call(bf16[16,4096]{1,0:T(8,128)(2,1)} %get-tuple-element.9.normed, bf16[4,256,128]{2,1,0:T(8,128)(2,1)} %get-tuple-element.10.meta_a, bf16[4,256,128]{2,1,0:T(8,128)(2,1)} %get-tuple-element.11.meta_b, f32[16,4096]{1,0:T(8,128)} %get-tuple-element.12.hidden, bf16[4096,384]{1,0:T(8,128)(2,1)} %bitcast.3, ...), custom_call_target="tpu_custom_call" | custom-call | tf_op jit(solution)/shard_map/moe/pallas_call | solution.py:553
  194.1 1.7 copy.15

commit v5 on v4

--- a/solution.py
+++ b/solution.py
@@ -17,7 +17,7 @@
 NT = (((1,), (1,)), ((), ()))
 ORDER = (0, 1, 3, 2)
 SPOS = {0: 0, 1: 1, 3: 2, 2: 3}
-MOE_SEMS = 104
+MOE_SEMS = 91
 FAR = (1, 2, 3)
 
 
@@ -597,7 +597,7 @@
     )(*operands)
 
 
-ATT_SEMS = 80
+ATT_SEMS = 75
 
 
 def attn_kernel(
@@ -1029,8 +1029,8 @@
     along_y(3, 1)
     for j in (1, 2, 3):
         along_x(j)
-    for j in range(4):
-        square = join(j, square)
+        square = join(j - 1, square)
+    square = join(3, square)
     mean = jnp.sum(square, -1, keepdims=True) * (1.0 / D)
     normed[...] = (hidden[...] * lax.rsqrt(mean + 1e-06) * gain_raw[...].reshape(1, D).astype(F32)).astype(BF)
     assert links.used <= ATT_SEMS

time: 196 us -> 196 us (level)
  no operation moved by 1% of the time
where the time goes in v5:
time: 196 us
  Pallas kernels  194 us (99%)
    pallas_call x1, Pallas kernels, moe(): pl.pallas_call(moe_kernel, out_shape=jax.ShapeDtypeStruct((8, 2, D), BF),...  131 us
    pallas_call x1, Pallas kernels, attention(): pl.pallas_call(attn_kernel, out_shape=(jax.ShapeDtypeStruct((16, D), F32)...  63.6 us

profile of v5, /device:TPU:1, one launch (start us, length us, event | category | flops | bytes accessed | tf_op | source)
XLA Modules:
  0.0 196.0 jit_solution(16370477498770734032)
XLA Ops:
  0.0 63.6 %attention.1 = (f32[16,4096]{1,0:T(8,128)}, bf16[16,4096]{1,0:T(8,128)(2,1)}, bf16[4,256,128]{2,1,0:T(8,128)(2,1)}, bf16[4,256,128]{2,1,0:T(8,128)(2,1)}) custom-call(bf16[128,2,512]{2,1,0:T(2,128)(2,1)} %queries.1, bf16[128,2,512]{2,1,0:T(2,128)(2,1)} %keys.1, bf16[128,2,512]{2,1,0:T(2,128)(2,1)} %values.1, bf16[64,512]{1,0:T(8,128)(2,1)} %prefix_keys.1, ...), custom_call_target="tpu_custom_call" | custom-call | tf_op jit(solution)/shard_map/attention/pallas_call | solution.py:1043
  63.6 130.7 %moe.1 = bf16[8,2,4096]{2,1,0:T(2,128)(2,1)} custom-call(bf16[16,4096]{1,0:T(8,128)(2,1)} %get-tuple-element.9.normed, bf16[4,256,128]{2,1,0:T(8,128)(2,1)} %get-tuple-element.10.meta_a, bf16[4,256,128]{2,1,0:T(8,128)(2,1)} %get-tuple-element.11.meta_b, f32[16,4096]{1,0:T(8,128)} %get-tuple-element.12.hidden, bf16[4096,384]{1,0:T(8,128)(2,1)} %bitcast.3, ...), custom_call_target="tpu_custom_call" | custom-call | tf_op jit(solution)/shard_map/moe/pallas_call | solution.py:553
  194.3 1.7 copy.15
